TPU v7x, 32 devices: a whole 2x2x4 slice. The times are simulated.
32 devices in a mesh: dp: 2 (over core), ctx: 16 (over z, y, x).
Axes of the slice: x: 2, y: 2, z: 4, core: 2. Of those that a mesh axis runs over, the one named last changes fastest.
Arguments:
- queries: bfloat16 [2, 2048, 2048], P('dp', 'ctx'), may hold values from -6 to 6
- keys: bfloat16 [2, 2048, 2048], P('dp', 'ctx'), may hold values from -6 to 6
- values: bfloat16 [2, 2048, 2048], P('dp', 'ctx'), may hold values from -6 to 6
- doc_ids: int32 [2, 32], P('dp', 'ctx'), may hold values from 0 to 7, never falling along the last dimension, each value on 1 to 8 neighbouring positions
- feat_weight: bfloat16 [128, 160], replicated, may hold values from -0.5 to 0.5
- out_grad: bfloat16 [2, 2048, 2048], P('dp', 'ctx'), may hold values from -6 to 6
Outputs:
- out: float32 [2, 2048, 2048], P('dp', 'ctx')
- query_grad: float32 [2, 2048, 2048], P('dp', 'ctx')
- key_grad: float32 [2, 2048, 2048], P('dp', 'ctx')
- value_grad: float32 [2, 2048, 2048], P('dp', 'ctx')
- new_weight: float32 [128, 160], replicated
Inputs may be any that keep to these rules, and one draw needn't show every extreme that they name: `doc_ids`: along each sequence the ids never fall; every id names one run of 1 to 8 blocks, and one run has exactly 8 blocks.
All inputs are finite; a program needn't handle non-finite values.
Results may differ from a plain program's by a relative error of at most 0.015.
Values sent between devices are 32-bit elements; how exact they have to be, the bound alone decides.
A program may use at most 64 MiB of HBM per device.

v0:
```python
import math

import jax
import jax.numpy as jnp
from jax import lax
from jax.sharding import PartitionSpec as P

H = 16
DH = 128
F = 160
BLOCK = 64


HIGH = lax.Precision.HIGHEST
RATE = 0.5
EPSILON = 1e-06


def passed_along(array, axis, by):
    length = lax.axis_size(axis)
    pairs = [(i, i + by) for i in range(length) if 0 <= i + by < length]
    return lax.ppermute(array, axis, pairs)


def features(proj):
    return (1.0 + proj + 0.5 * proj * proj).astype(jnp.bfloat16)


def pack_parts(parts):
    return jnp.concatenate([part.reshape(-1) for part in parts])


def unpack_parts(packed, shapes):
    result = []
    offset = 0
    for shape in shapes:
        length = math.prod(shape)
        result.append(packed[offset : offset + length].reshape(shape))
        offset = offset + length
    return result


def chain_combine(earlier, later):
    joined = later[0] == earlier[0]
    merged = later[1:] + jnp.where(joined, earlier[1:], jnp.zeros_like(earlier[1:]))
    return jnp.concatenate([later[:1], merged])


def prefix(packed, reverse, mover):
    count = lax.axis_size("ctx")
    index = lax.axis_index("ctx")
    blank = jnp.zeros_like(packed).at[0].set(-1.0)
    sign = -1 if reverse else 1

    def valid(step):
        if reverse:
            return index < count - step
        return index >= step

    total = jnp.where(valid(1), mover(packed, sign), blank)
    step = 1
    while step < count:
        got = mover(total, sign * step)
        total = jnp.where(valid(step), chain_combine(got, total), total)
        step = step * 2
    return total


def norm_mover(value, by):
    return passed_along(value, "ctx", by)


def value_mover(value, by):
    return passed_along(value, "ctx", by)


def back_mover(value, by):
    return passed_along(value, "ctx", by)


def back_norm_mover(value, by):
    return passed_along(value, "ctx", by)


def shards(queries, keys, values, doc_ids, feat_weight, out_grad):
    tokens = queries.shape[1]
    query3 = queries.reshape(tokens, H, DH)
    key3 = keys.reshape(tokens, H, DH)
    value3 = values.reshape(tokens, H, DH)
    grad3 = out_grad.reshape(tokens, H, DH).astype(jnp.float32)
    blocks = doc_ids.shape[1]
    docs = jnp.broadcast_to(doc_ids[0][:, None], (blocks, BLOCK)).reshape(tokens)
    doc_float = docs.astype(jnp.float32)
    proj_q = jnp.einsum("thd,df->thf", query3, feat_weight, preferred_element_type=jnp.float32)
    proj_k = jnp.einsum("thd,df->thf", key3, feat_weight, preferred_element_type=jnp.float32)
    feat_q = features(proj_q)
    feat_k = features(proj_k)
    order = jnp.arange(tokens)
    mask = jnp.logical_and(order[None, :] <= order[:, None], docs[None, :] == docs[:, None]).astype(
        jnp.float32
    )
    raw = jnp.einsum("thf,shf->hts", feat_q, feat_k, preferred_element_type=jnp.float32)
    probs = (raw * mask[None]).astype(jnp.bfloat16)
    num_local = jnp.einsum("hts,shd->thd", probs, value3, preferred_element_type=jnp.float32)
    den_local = jnp.sum(probs, axis=2, dtype=jnp.float32).T
    feat_qf = feat_q.astype(jnp.float32)
    feat_kf = feat_k.astype(jnp.float32)
    value_f = value3.astype(jnp.float32)
    tail_mask = (docs == docs[-1]).astype(jnp.float32)
    head_mask = (docs == docs[0]).astype(jnp.float32)
    tail_state = jnp.einsum(
        "thf,thd->hfd",
        feat_k * tail_mask.astype(jnp.bfloat16)[:, None, None],
        value3,
        preferred_element_type=jnp.float32,
    )
    tail_norm = jnp.einsum("thf,t->hf", feat_kf, tail_mask, precision=HIGH)
    last_doc = doc_float[-1:]
    first_doc = doc_float[:1]
    head_feat = feat_qf * head_mask[:, None, None]
    state_shape = (H, F, DH)
    norm_shape = (H, F)
    norm_sums = prefix(pack_parts([last_doc, tail_norm]), False, norm_mover)
    pre_doc, norm_in = unpack_parts(norm_sums, [(1,), norm_shape])
    pre_end = pre_doc[0]
    in_mask = (doc_float == pre_end).astype(jnp.float32)
    den = den_local + jnp.einsum("thf,hf->th", feat_qf, norm_in, precision=HIGH) * in_mask[:, None]
    scaled = grad3 / den[:, :, None]
    head_state = jnp.einsum("thf,thd->hfd", head_feat, scaled, precision=HIGH)
    in_mask, den, scaled, head_state = (in_mask, den, scaled, head_state)
    state_sums = prefix(pack_parts([last_doc, tail_state]), False, value_mover)
    state_in = unpack_parts(state_sums, [(1,), state_shape])[1]
    adjoint_sums = prefix(pack_parts([first_doc, head_state]), True, back_mover)
    post_doc, adjoint = unpack_parts(adjoint_sums, [(1,), state_shape])
    suffix_doc = post_doc[0]
    out = (
        num_local
        + jnp.einsum("thf,hfd->thd", feat_qf, state_in, precision=HIGH) * in_mask[:, None, None]
    ) / den[:, :, None]
    drift = -jnp.sum(grad3 * out, axis=2) / den
    head_norm = jnp.einsum("thf,th->hf", head_feat, drift, precision=HIGH)
    out, drift, head_norm = (out, drift, head_norm)
    drift_sums = prefix(pack_parts([first_doc, head_norm]), True, back_norm_mover)
    adjoint_norm = unpack_parts(drift_sums, [(1,), norm_shape])[1]
    scaled_b = scaled.astype(jnp.bfloat16)
    dscore = (
        jnp.einsum("thd,shd->hts", scaled_b, value3, preferred_element_type=jnp.float32)
        + drift.T[:, :, None]
    )
    dprobs = (dscore * mask[None]).astype(jnp.bfloat16)
    out_mask = (doc_float == suffix_doc).astype(jnp.float32)
    grad_fq = (
        jnp.einsum("hts,shf->thf", dprobs, feat_k, preferred_element_type=jnp.float32)
        + (
            jnp.einsum("hfd,thd->thf", state_in, scaled, precision=HIGH)
            + norm_in[None] * drift[:, :, None]
        )
        * in_mask[:, None, None]
    )
    grad_fk = (
        jnp.einsum("hts,thf->shf", dprobs, feat_q, preferred_element_type=jnp.float32)
        + (jnp.einsum("hfd,shd->shf", adjoint, value_f, precision=HIGH) + adjoint_norm[None])
        * out_mask[:, None, None]
    )
    value_grad = (
        jnp.einsum("hts,thd->shd", probs, scaled_b, preferred_element_type=jnp.float32)
        + jnp.einsum("shf,hfd->shd", feat_kf, adjoint, precision=HIGH) * out_mask[:, None, None]
    )
    grad_pq = (grad_fq * (1.0 + proj_q)).astype(jnp.bfloat16)
    grad_pk = (grad_fk * (1.0 + proj_k)).astype(jnp.bfloat16)
    query_grad = jnp.einsum("thf,df->thd", grad_pq, feat_weight, preferred_element_type=jnp.float32)
    key_grad = jnp.einsum("thf,df->thd", grad_pk, feat_weight, preferred_element_type=jnp.float32)
    weight_part = jnp.einsum(
        "thd,thf->df", query3, grad_pq, preferred_element_type=jnp.float32
    ) + jnp.einsum("thd,thf->df", key3, grad_pk, preferred_element_type=jnp.float32)
    weight_grad = lax.psum(weight_part, ("dp", "ctx"))
    scale = lax.rsqrt(jnp.mean(weight_grad * weight_grad) + EPSILON)
    new_weight = feat_weight.astype(jnp.float32) - RATE * weight_grad * scale
    shape_out = (1, tokens, H * DH)
    return (
        out.reshape(shape_out),
        query_grad.reshape(shape_out),
        key_grad.reshape(shape_out),
        value_grad.reshape(shape_out),
        new_weight,
    )


def solution(mesh):
    placed = (
        P("dp", "ctx", None),
        P("dp", "ctx", None),
        P("dp", "ctx", None),
        P("dp", "ctx"),
        P(),
        P("dp", "ctx", None),
    )
    return jax.shard_map(
        shards,
        mesh=mesh,
        in_specs=placed,
        out_specs=(
            P("dp", "ctx", None),
            P("dp", "ctx", None),
            P("dp", "ctx", None),
            P("dp", "ctx", None),
            P(),
        ),
        check_vma=False,
    )
```

profile of v0, /device:TPU:0, one launch (start us, length us, event | category | flops | bytes accessed | tf_op | source)
XLA Modules:
  0.0 576.7 jit_solution(12221369019242952818)
XLA Ops:
  8.6 1.3 broadcast_compare_fusion
  10.1 1.1 copy.46
  11.9 1.2 fusion.20
  14.1 4.8 collective-permute-start.5
  19.1 1.2 collective-permute-done.5
  20.4 4.2 collective-permute-start.6
  24.6 1.4 fusion.16
  29.2 5.4 collective-permute-start.7
  38.6 6.9 %collective-permute-start.8 = (f32[2561]{0:T(1024)S(1)}, f32[2561]{0:T(1024)S(1)}, u32[]{:S(2)}, u32[]{:S(2)}) collective-permute-start(f32[2561]{0:T(1024)S(1)} %maximum_select_fusion.8), channel_id=1, source_target_pairs={{0,4},{1,5},{2,6},{3,7},{4,8},{5,9},{6,10},{7,11},{8,12},{9,13},{1... | collective-permute-start | bytes 30740 | tf_op jit(solution)/shard_map/ppermute | solution.py:22
  49.5 5.2 collective-permute-start.9
  54.7 1.3 convert_reduce_fusion
  56.2 1.2 copy.16
  61.0 1.9 compare_convert_fusion.1
  63.3 2.0 pad_maximum_fusion
  65.3 2.4 collective-permute-start
  68.4 3.5 fusion.31
  72.0 2.1 pad_maximum_fusion.1
  74.1 1.3 collective-permute-start.10
  75.4 43.2 %collective-permute-done = f32[327681]{0:T(1024)} collective-permute-done((f32[327681]{0:T(1024)}, f32[327681]{0:T(1024)}, u32[]{:S(2)}, u32[]{:S(2)}) %collective-permute-start) | collective-permute-done | bytes 1310756 | tf_op jit(solution)/shard_map/ppermute | solution.py:22
  118.6 2.3 collective-permute-done.10
  122.0 4.4 collective-permute-start.1
  126.4 1.3 collective-permute-start.11
  128.8 48.3 %collective-permute-done.1 = f32[327681]{0:T(1024)S(1)} collective-permute-done((f32[327681]{0:T(1024)S(1)}, f32[327681]{0:T(1024)S(1)}, u32[]{:S(2)}, u32[]{:S(2)}) %collective-permute-start.1) | collective-permute-done | bytes 1310756 | tf_op jit(solution)/shard_map/ppermute | solution.py:22
  183.2 2.1 maximum_select_fusion.3
  185.3 2.4 collective-permute-start.2
  187.8 2.8 fusion.51
  191.2 1.3 collective-permute-start.12
  193.0 17.9 %collective-permute-done.2 = f32[327681]{0:T(1024)} collective-permute-done((f32[327681]{0:T(1024)S(1)}, f32[327681]{0:T(1024)}, u32[]{:S(2)}, u32[]{:S(2)}) %collective-permute-start.2) | collective-permute-done | bytes 1310756 | tf_op jit(solution)/shard_map/ppermute | solution.py:22
  210.9 1.2 slice.346
  213.3 2.1 fusion.28
  216.5 72.6 %collective-permute-start.3 = (f32[327681]{0:T(1024)S(1)}, f32[327681]{0:T(1024)S(1)}, u32[]{:S(2)}, u32[]{:S(2)}) collective-permute-start(f32[327681]{0:T(1024)S(1)} %maximum_select_fusion.1), channel_id=1, source_target_pairs={{0,4},{1,5},{2,6},{3,7},{4,8},{5,9},{6,10},{7,11},{8,12},{9,13},{1... | collective-permute-start | bytes 3932180 | tf_op jit(solution)/shard_map/ppermute | solution.py:22
  293.3 1.3 collective-permute-start.13
  295.1 20.6 %collective-permute-done.3 = f32[327681]{0:T(1024)S(1)} collective-permute-done((f32[327681]{0:T(1024)S(1)}, f32[327681]{0:T(1024)S(1)}, u32[]{:S(2)}, u32[]{:S(2)}) %collective-permute-start.3) | collective-permute-done | bytes 1310756 | tf_op jit(solution)/shard_map/ppermute | solution.py:22
  319.3 4.2 collective-permute-start.4
  328.1 1.3 collective-permute-start.14
  329.9 19.7 %collective-permute-done.4 = f32[327681]{0:T(1024)S(1)} collective-permute-done((f32[327681]{0:T(1024)S(1)}, f32[327681]{0:T(1024)S(1)}, u32[]{:S(2)}, u32[]{:S(2)}) %collective-permute-start.4) | collective-permute-done | bytes 1310756 | tf_op jit(solution)/shard_map/ppermute | solution.py:22
  352.2 1.1 fusion.25
  353.4 1.9 fusion.12
  355.3 1.4 multiply_reduce_fusion
  356.7 2.1 fusion.30
  359.6 1.3 collective-permute-start.15
  360.9 1.7 fusion.32
  362.8 1.5 fusion.7
  364.4 22.9 %collective-permute-done.14 = f32[327681]{0:T(1024)} collective-permute-done((f32[327681]{0:T(1024)S(1)}, f32[327681]{0:T(1024)}, u32[]{:S(2)}, u32[]{:S(2)}) %collective-permute-start.14) | collective-permute-done | bytes 1310756 | tf_op jit(solution)/shard_map/ppermute | solution.py:22
  387.3 1.2 slice.389
  389.7 2.1 fusion.21
  394.0 1.5 collective-permute-start.16
  397.1 2.5 collective-permute-done.16
  402.2 1.3 collective-permute-start.17
  403.5 2.8 fusion.11
  406.8 1.4 collective-permute-done.17
  410.8 1.3 collective-permute-start.18
  412.1 1.6 fusion.76
  414.3 5.8 collective-permute-done.18
  422.6 1.3 collective-permute-start.19
  423.9 1.3 fusion.58
  425.2 2.6 copy.31
  427.9 1.3 copy.29
  429.2 2.6 copy.28
  435.0 2.9 fusion.13
  440.5 1.3 copy.30
  441.8 124.3 %all-reduce.2.cloned.1.call-done = f32[128,160]{0,1:T(8,128)} async-done(((f32[128,160]{0,1:T(8,128)}), f32[128,160]{0,1:T(8,128)}) %all-reduce.2.cloned.1.call-update) | async-done | bytes 81936 | tf_op jit(solution)/shard_map/psum | solution.py:176
  566.1 1.5 multiply_reduce_fusion.1
  568.3 1.5 multiply_subtract_fusion
  (162 shorter events, 47.3 us)
Async XLA Ops:
  7.2 558.9 %all-reduce.2.cloned.1.call-start = ((), (), s32[]{:S(2)}) async-start(), calls=%async_computation | async-start | bytes 163840 | tf_op jit(solution)/shard_map/psum | solution.py:176
  11.2 2.3 copy-start.13
  11.9 7.1 %copy-start.25 = (bf16[1,128,2048]{2,1,0:T(8,128)(2,1)S(1)}, bf16[1,128,2048]{2,1,0:T(8,128)(2,1)}, u32[]{:S(2)}) copy-start(bf16[1,128,2048]{2,1,0:T(8,128)(2,1)} %param.14) | copy-start | bytes 1572868
  13.2 21.4 %copy-start = (f32[128,16,160]{0,2,1:T(8,128)}, f32[128,16,160]{0,2,1:T(8,128)S(1)}, u32[]{:S(2)}) copy-start(f32[128,16,160]{0,2,1:T(8,128)S(1)} %get-tuple-element.64) | copy-start | bytes 3932164
  13.2 7.2 %copy-start.28 = (f32[2561]{0:T(1024)S(1)}, f32[2561]{0:T(1024)}, u32[]{:S(2)}) copy-start(f32[2561]{0:T(1024)} %constant.104.clone.1) | copy-start | bytes 30736
  13.2 11.4 %copy-start.23 = (bf16[128,160]{0,1:T(8,128)(2,1)S(1)}, bf16[128,160]{0,1:T(8,128)(2,1)}, u32[]{:S(2)}) copy-start(bf16[128,160]{0,1:T(8,128)(2,1)} %param.18) | copy-start | bytes 122884
  14.1 6.2 %collective-permute-start.5 = (f32[2561]{0:T(1024)S(1)}, f32[2561]{0:T(1024)S(1)}, u32[]{:S(2)}, u32[]{:S(2)}) collective-permute-start(f32[2561]{0:T(1024)S(1)} %pad_maximum_fusion.4), channel_id=1, source_target_pairs={{0,1},{1,2},{2,3},{3,4},{4,5},{5,6},{6,7},{7,8},{8,9},{9,10},{10,1... | collective-permute-start | bytes 30740 | tf_op jit(solution)/shard_map/ppermute | solution.py:22
  19.1 10.1 %copy-start.15 = (bf16[16,8,16,128]{3,2,1,0:T(8,128)(2,1)}, bf16[16,8,16,128]{3,2,1,0:T(8,128)(2,1)S(1)}, u32[]{:S(2)}) copy-start(bf16[16,8,16,128]{3,2,1,0:T(8,128)(2,1)S(1)} %copy.45) | copy-start | bytes 1572868
  20.4 6.2 %collective-permute-start.6 = (f32[2561]{0:T(1024)S(1)}, f32[2561]{0:T(1024)S(1)}, u32[]{:S(2)}, u32[]{:S(2)}) collective-permute-start(f32[2561]{0:T(1024)S(1)} %broadcast_select_fusion.3), channel_id=1, source_target_pairs={{0,1},{1,2},{2,3},{3,4},{4,5},{5,6},{6,7},{7,8},{8,9},{9,10},{10,1... | collective-permute-start | bytes 30740 | tf_op jit(solution)/shard_map/ppermute | solution.py:22
  26.0 42.4 %copy-start.2 = (bf16[128,16,160]{0,2,1:T(8,128)(2,1)}, bf16[128,16,160]{0,2,1:T(8,128)(2,1)S(1)}, u32[]{:S(2)}) copy-start(bf16[128,16,160]{0,2,1:T(8,128)(2,1)S(1)} %get-tuple-element.61) | copy-start | bytes 1966084
  29.2 6.8 %collective-permute-start.7 = (f32[2561]{0:T(1024)S(1)}, f32[2561]{0:T(1024)S(1)}, u32[]{:S(2)}, u32[]{:S(2)}) collective-permute-start(f32[2561]{0:T(1024)S(1)} %maximum_select_fusion.7), channel_id=1, source_target_pairs={{0,2},{1,3},{2,4},{3,5},{4,6},{5,7},{6,8},{7,9},{8,10},{9,11},{10,... | collective-permute-start | bytes 30740 | tf_op jit(solution)/shard_map/ppermute | solution.py:22
  34.8 21.2 %copy-start.26 = (bf16[1,128,2048]{2,1,0:T(8,128)(2,1)S(1)}, bf16[1,128,2048]{2,1,0:T(8,128)(2,1)}, u32[]{:S(2)}) copy-start(bf16[1,128,2048]{2,1,0:T(8,128)(2,1)} %param.16) | copy-start | bytes 1572868
  38.6 8.3 %collective-permute-start.8 = (f32[2561]{0:T(1024)S(1)}, f32[2561]{0:T(1024)S(1)}, u32[]{:S(2)}, u32[]{:S(2)}) collective-permute-start(f32[2561]{0:T(1024)S(1)} %maximum_select_fusion.8), channel_id=1, source_target_pairs={{0,4},{1,5},{2,6},{3,7},{4,8},{5,9},{6,10},{7,11},{8,12},{9,13},{1... | collective-permute-start | bytes 30740 | tf_op jit(solution)/shard_map/ppermute | solution.py:22
  49.5 8.4 %collective-permute-start.9 = (f32[2561]{0:T(1024)S(1)}, f32[2561]{0:T(1024)S(1)}, u32[]{:S(2)}, u32[]{:S(2)}) collective-permute-start(f32[2561]{0:T(1024)S(1)} %maximum_select_fusion.9), channel_id=1, source_target_pairs={{0,8},{1,9},{2,10},{3,11},{4,12},{5,13},{6,14},{7,15},{16,24},{17,... | collective-permute-start | bytes 30740 | tf_op jit(solution)/shard_map/ppermute | solution.py:22
  54.7 1.4 copy-start.24
  56.2 15.8 %copy-start.17 = (bf16[16,8,16,128]{3,2,1,0:T(8,128)(2,1)}, bf16[16,8,16,128]{3,2,1,0:T(8,128)(2,1)S(1)}, u32[]{:S(2)}) copy-start(bf16[16,8,16,128]{3,2,1,0:T(8,128)(2,1)S(1)} %copy.44) | copy-start | bytes 1572868
  65.3 53.3 %collective-permute-start = (f32[327681]{0:T(1024)}, f32[327681]{0:T(1024)}, u32[]{:S(2)}, u32[]{:S(2)}) collective-permute-start(f32[327681]{0:T(1024)} %pad_maximum_fusion), channel_id=1, source_target_pairs={{0,1},{1,2},{2,3},{3,4},{4,5},{5,6},{6,7},{7,8},{8,9},{9,10},{10,1... | collective-permute-start | bytes 3932180 | tf_op jit(solution)/shard_map/ppermute | solution.py:22
  72.0 48.9 %copy-start.6 = (f32[327681]{0:T(1024)S(1)}, f32[327681]{0:T(1024)}, u32[]{:S(2)}) copy-start(f32[327681]{0:T(1024)} %constant.102.clone.1) | copy-start | bytes 3932176
  74.1 46.8 %collective-permute-start.10 = (f32[327681]{0:T(1024)}, f32[327681]{0:T(1024)S(1)}, u32[]{:S(2)}, u32[]{:S(2)}) collective-permute-start(f32[327681]{0:T(1024)} %pad_maximum_fusion.1), channel_id=1, source_target_pairs={{1,0},{2,1},{3,2},{4,3},{5,4},{6,5},{7,6},{8,7},{9,8},{10,9},{11,1... | collective-permute-start | bytes 3932180 | tf_op jit(solution)/shard_map/ppermute | solution.py:22
  120.9 1.1 copy-start.8
  122.0 55.1 %collective-permute-start.1 = (f32[327681]{0:T(1024)S(1)}, f32[327681]{0:T(1024)S(1)}, u32[]{:S(2)}, u32[]{:S(2)}) collective-permute-start(f32[327681]{0:T(1024)S(1)} %get-tuple-element.53), channel_id=1, source_target_pairs={{0,1},{1,2},{2,3},{3,4},{4,5},{5,6},{6,7},{7,8},{8,9},{9,10},{10,1... | collective-permute-start | bytes 3932180 | tf_op jit(solution)/shard_map/ppermute | solution.py:22
  126.4 52.5 %collective-permute-start.11 = (f32[327681]{0:T(1024)S(1)}, f32[327681]{0:T(1024)S(1)}, u32[]{:S(2)}, u32[]{:S(2)}) collective-permute-start(f32[327681]{0:T(1024)S(1)} %get-tuple-element.52), channel_id=1, source_target_pairs={{1,0},{2,1},{3,2},{4,3},{5,4},{6,5},{7,6},{8,7},{9,8},{10,9},{11,1... | collective-permute-start | bytes 3932180 | tf_op jit(solution)/shard_map/ppermute | solution.py:22
  181.5 1.3 copy-start.7
  181.5 1.7 copy-start.9
  185.3 25.5 %collective-permute-start.2 = (f32[327681]{0:T(1024)S(1)}, f32[327681]{0:T(1024)}, u32[]{:S(2)}, u32[]{:S(2)}) collective-permute-start(f32[327681]{0:T(1024)S(1)} %get-tuple-element.51), channel_id=1, source_target_pairs={{0,2},{1,3},{2,4},{3,5},{4,6},{5,7},{6,8},{7,9},{8,10},{9,11},{10,... | collective-permute-start | bytes 3932180 | tf_op jit(solution)/shard_map/ppermute | solution.py:22
  191.2 97.9 %collective-permute-start.12 = (f32[327681]{0:T(1024)S(1)}, f32[327681]{0:T(1024)S(1)}, u32[]{:S(2)}, u32[]{:S(2)}) collective-permute-start(f32[327681]{0:T(1024)S(1)} %get-tuple-element.50), channel_id=1, source_target_pairs={{2,0},{3,1},{4,2},{5,3},{6,4},{7,5},{8,6},{9,7},{10,8},{11,9},{12,... | collective-permute-start | bytes 3932180 | tf_op jit(solution)/shard_map/ppermute | solution.py:22
  216.5 99.2 %collective-permute-start.3 = (f32[327681]{0:T(1024)S(1)}, f32[327681]{0:T(1024)S(1)}, u32[]{:S(2)}, u32[]{:S(2)}) collective-permute-start(f32[327681]{0:T(1024)S(1)} %maximum_select_fusion.1), channel_id=1, source_target_pairs={{0,4},{1,5},{2,6},{3,7},{4,8},{5,9},{6,10},{7,11},{8,12},{9,13},{1... | collective-permute-start | bytes 3932180 | tf_op jit(solution)/shard_map/ppermute | solution.py:22
  293.3 30.9 %collective-permute-start.13 = (f32[327681]{0:T(1024)S(1)}, f32[327681]{0:T(1024)S(1)}, u32[]{:S(2)}, u32[]{:S(2)}) collective-permute-start(f32[327681]{0:T(1024)S(1)} %maximum_select_fusion.4), channel_id=1, source_target_pairs={{4,0},{5,1},{6,2},{7,3},{8,4},{9,5},{10,6},{11,7},{12,8},{13,9},{1... | collective-permute-start | bytes 3932180 | tf_op jit(solution)/shard_map/ppermute | solution.py:22
  319.3 30.3 %collective-permute-start.4 = (f32[327681]{0:T(1024)S(1)}, f32[327681]{0:T(1024)S(1)}, u32[]{:S(2)}, u32[]{:S(2)}) collective-permute-start(f32[327681]{0:T(1024)S(1)} %maximum_select_fusion.2), channel_id=1, source_target_pairs={{0,8},{1,9},{2,10},{3,11},{4,12},{5,13},{6,14},{7,15},{16,24},{17,... | collective-permute-start | bytes 3932180 | tf_op jit(solution)/shard_map/ppermute | solution.py:22
  328.1 59.2 %collective-permute-start.14 = (f32[327681]{0:T(1024)S(1)}, f32[327681]{0:T(1024)}, u32[]{:S(2)}, u32[]{:S(2)}) collective-permute-start(f32[327681]{0:T(1024)S(1)} %maximum_select_fusion.5), channel_id=1, source_target_pairs={{8,0},{9,1},{10,2},{11,3},{12,4},{13,5},{14,6},{15,7},{24,16},{25,... | collective-permute-start | bytes 3932180 | tf_op jit(solution)/shard_map/ppermute | solution.py:22
  352.2 1.1 copy-start.3
  353.3 2.0 copy-start.10
  353.4 1.9 copy-start.18
  353.4 1.9 copy-start.20
  353.4 2.0 copy-start.27
  359.6 34.4 %collective-permute-start.15 = (f32[2561]{0:T(1024)S(1)}, f32[2561]{0:T(1024)S(1)}, u32[]{:S(2)}, u32[]{:S(2)}) collective-permute-start(f32[2561]{0:T(1024)S(1)} %pad_maximum_fusion.5), channel_id=1, source_target_pairs={{1,0},{2,1},{3,2},{4,3},{5,4},{6,5},{7,6},{8,7},{9,8},{10,9},{11,1... | collective-permute-start | bytes 30740 | tf_op jit(solution)/shard_map/ppermute | solution.py:22
  360.9 1.7 copy-start.11
  360.9 1.9 copy-start.21
  391.8 1.3 copy-start.12
  393.4 30.5 %copy-start.4 = (bf16[128,16,160]{0,2,1:T(8,128)(2,1)}, bf16[128,16,160]{0,2,1:T(8,128)(2,1)S(1)}, u32[]{:S(2)}) copy-start(bf16[128,16,160]{0,2,1:T(8,128)(2,1)S(1)} %fusion.14) | copy-start | bytes 1966084
  394.0 5.6 collective-permute-start.16
  396.2 7.3 %copy-start.22 = (f32[16,128,128]{2,1,0:T(8,128)S(1)}, f32[16,128,128]{2,1,0:T(8,128)}, u32[]{:S(2)}) copy-start(f32[16,128,128]{2,1,0:T(8,128)} %fusion.51) | copy-start | bytes 3145732
  402.2 6.1 %collective-permute-start.17 = (f32[2561]{0:T(1024)S(1)}, f32[2561]{0:T(1024)S(1)}, u32[]{:S(2)}, u32[]{:S(2)}) collective-permute-start(f32[2561]{0:T(1024)S(1)} %maximum_select_fusion.11), channel_id=1, source_target_pairs={{2,0},{3,1},{4,2},{5,3},{6,4},{7,5},{8,6},{9,7},{10,8},{11,9},{12,... | collective-permute-start | bytes 30740 | tf_op jit(solution)/shard_map/ppermute | solution.py:22
  410.8 9.2 %collective-permute-start.18 = (f32[2561]{0:T(1024)S(1)}, f32[2561]{0:T(1024)S(1)}, u32[]{:S(2)}, u32[]{:S(2)}) collective-permute-start(f32[2561]{0:T(1024)S(1)} %maximum_select_fusion.12), channel_id=1, source_target_pairs={{4,0},{5,1},{6,2},{7,3},{8,4},{9,5},{10,6},{11,7},{12,8},{13,9},{1... | collective-permute-start | bytes 30740 | tf_op jit(solution)/shard_map/ppermute | solution.py:22
  422.6 9.7 %collective-permute-start.19 = (f32[2561]{0:T(1024)S(1)}, f32[2561]{0:T(1024)S(1)}, u32[]{:S(2)}, u32[]{:S(2)}) collective-permute-start(f32[2561]{0:T(1024)S(1)} %maximum_select_fusion.13), channel_id=1, source_target_pairs={{8,0},{9,1},{10,2},{11,3},{12,4},{13,5},{14,6},{15,7},{24,16},{25,... | collective-permute-start | bytes 30740 | tf_op jit(solution)/shard_map/ppermute | solution.py:22
  425.2 2.6 copy-start.19
  429.2 5.8 %copy-start.1 = (f32[128,16,160]{0,2,1:T(8,128)S(1)}, f32[128,16,160]{0,2,1:T(8,128)}, u32[]{:S(2)}) copy-start(f32[128,16,160]{0,2,1:T(8,128)} %copy-done) | copy-start | bytes 3932164
  435.0 2.9 copy-start.14
  437.9 1.1 copy-start.5
  437.9 1.2 copy-start.16
Sparse Core Ops, SparseCore 0:
  440.2 125.7 all-reduce.1
where the time goes:
time: 580 us; the launch traced here: 577 us
  waiting for transfers between devices  312 us (54%)
  starting transfers between devices  126 us (22%)
  other arithmetic  36.5 us (6%)
  between operations  35.9 us (6%)
  local copies, waits for them, and re-layouts  35.8 us (6%)
  matrix products  30.7 us (5%)
    ppermute x20, waiting for transfers between devices, passed_along(): return lax.ppermute(array, axis, pairs)  188 us
    ppermute x20, starting transfers between devices, passed_along(): return lax.ppermute(array, axis, pairs)  126 us
    psum x1, waiting for transfers between devices, shards(): weight_grad = lax.psum(weight_part, ('dp', 'ctx'))  124 us
    select_n x15, other arithmetic, prefix(): total = jnp.where(valid(step), chain_combine(got, total), total)  14.2 us
    unnamed x65, local copies, waits for them, and re-layouts  12.5 us
  transfers between devices with their start and end apart: 21, of which 15 were waited for; matrix products, arithmetic and copies ran while one was open for 11% of the time, Pallas kernels for 0%

commit v1 on v0

v1 whole, which is shorter than its diff:
```python
import functools

import jax
import jax.numpy as jnp
from jax import lax
from jax.experimental import pallas as pl
from jax.experimental.pallas import tpu as pltpu
from jax.sharding import PartitionSpec as P

H = 16
DH = 128
F = 160
BLOCK = 64
RATE = 0.5
EPSILON = 1e-06
STEP = 4
CHUNK = 4
MESH = pl.DeviceIdType.MESH
BF = jnp.bfloat16
F32 = jnp.float32
LIMIT = 56 * 1024 * 1024


def dot(a, b, dims):
    return lax.dot_general(a, b, ((dims[:1], dims[1:]), ((), ())), preferred_element_type=F32)


def features(proj):
    return (1.0 + proj + 0.5 * proj * proj).astype(BF)


def halves(x):
    high = x.astype(BF)
    return high, (x - high.astype(F32)).astype(BF)


def row_docs(doc_ref, shape, dim):
    place = lax.broadcasted_iota(jnp.int32, shape, dim) // BLOCK
    docs = jnp.zeros(shape, F32)
    for block in range(doc_ref.shape[1]):
        docs = jnp.where(place == block, doc_ref[0, block].astype(F32), docs)
    return docs


def same(a, b):
    return jnp.where(a == b, 1.0, 0.0)


def head_columns(head):
    return pl.ds(pl.multiple_of(head * DH, DH), DH)


def local_kernel(doc_ref, q_ref, k_ref, v_ref, w_ref, fq_ref, probs_ref, state_ref, norm_ref, den_ref):
    tokens = q_ref.shape[0]
    rows = row_docs(doc_ref, (tokens, 1), 0)
    mask = jnp.logical_and(
        lax.broadcasted_iota(jnp.int32, (tokens, tokens), 1)
        <= lax.broadcasted_iota(jnp.int32, (tokens, tokens), 0),
        rows == row_docs(doc_ref, (1, tokens), 1),
    )
    tail = same(rows, doc_ref[0, doc_ref.shape[1] - 1].astype(F32))
    weight = w_ref[...]
    ones = jnp.ones((tokens, DH), BF)
    norms = []
    for j in range(STEP):
        part = slice(j * DH, (j + 1) * DH)
        value = v_ref[:, part]
        feat_q = features(dot(q_ref[:, part], weight, (1, 0)))
        feat_k = features(dot(k_ref[:, part], weight, (1, 0)))
        probs = jnp.where(mask, dot(feat_q, feat_k, (1, 1)), 0.0).astype(BF)
        tail_k = feat_k.astype(F32) * tail
        fq_ref[j] = feat_q
        probs_ref[j] = probs
        den_ref[:, part] = dot(probs, ones, (1, 0))
        state_ref[j] = dot(tail_k.astype(BF), value, (0, 0))
        norms.append(jnp.sum(tail_k, axis=0, keepdims=True))
    for j in range(STEP):
        norm_ref[j] = jnp.concatenate([norms[j], jnp.zeros((1, 256 - F), F32)], axis=1)


def bits(count):
    return [1 << r for r in range(count.bit_length() - 1)]


def exchange_kernel(
    n, group, doc_ref, fq_ref, state_ref, norm_ref, den0_ref, g_ref,
    s_ref, a_ref, nin_ref, den_ref, edge_ref,
    msg, note, table, got_msg, got_note, adj, part, suffix, got,
    ms, mr, ns, nr, send, recv,
):
    me = lax.axis_index("ctx")
    rounds = bits(group)
    last_round = len(rounds)
    chunks = H // CHUNK

    barrier = pltpu.get_barrier_semaphore()
    for k in range(1, group + 1):
        for target in (lax.rem(me + k, n), lax.rem(me + n - k, n)):
            pl.semaphore_signal(barrier, inc=1, device_id={"ctx": target}, device_id_type=MESH)

    last = doc_ref[0, doc_ref.shape[1] - 1].astype(F32)
    first = doc_ref[0, 0].astype(F32)
    which = lax.broadcasted_iota(jnp.int32, (8, 256), 0)
    tile = jnp.where(which == 0, last, jnp.where(which == 1, first, 0.0))
    note[...] = tile
    table[group] = tile
    for h in range(H):
        msg[h : h + 1, :] = norm_ref[h]
    msg[H : H + 8, :] = tile
    pl.semaphore_wait(barrier, 2 * group)

    small = []
    for k in range(1, group + 1):
        small.append(pltpu.make_async_remote_copy(
            src_ref=msg, dst_ref=got_msg.at[k - 1], send_sem=ms.at[k - 1], recv_sem=mr.at[k - 1],
            device_id={"ctx": lax.rem(me + k, n)}, device_id_type=MESH))
        small.append(pltpu.make_async_remote_copy(
            src_ref=note, dst_ref=got_note.at[k - 1], send_sem=ns.at[k - 1], recv_sem=nr.at[k - 1],
            device_id={"ctx": lax.rem(me + n - k, n)}, device_id_type=MESH))
    for copy in small:
        copy.start()

    def copy_of(kind, c, r):
        heads = pl.ds(c * CHUNK, CHUNK)
        if r < last_round:
            b = rounds[r]
            target = me + b - 2 * b * lax.rem(me // b, 2)
        else:
            target = me + group if kind == 0 else me - group
        if r == 0 and last_round > 0:
            source = (state_ref if kind == 0 else adj).at[heads]
        elif r < last_round:
            source = part.at[kind, r - 1, heads]
        else:
            source = suffix.at[kind, heads]
        slot = (kind * chunks + c) * (last_round + 1) + r
        return pltpu.make_async_remote_copy(
            src_ref=source, dst_ref=got.at[kind, r, heads], send_sem=send.at[slot], recv_sem=recv.at[slot],
            device_id={"ctx": target}, device_id_type=MESH)

    can_up = me + group < n
    can_down = me >= group

    def start(kind, c, r):
        if r < last_round:
            copy_of(kind, c, r).start()
        else:
            @pl.when(can_up if kind == 0 else can_down)
            def _():
                copy_of(kind, c, r).start()

    for c in range(chunks):
        start(0, c, 0)

    for k in range(group):
        small[2 * k].wait_recv()
        small[2 * k + 1].wait_recv()
    for k in range(1, group + 1):
        table[group - k] = got_msg[k - 1, H : H + 8, :]
        table[group + k] = got_note[k - 1]

    def doc_at(index, kind):
        return table[index - me + group][kind : kind + 1, :]

    before = table[group - 1][0:1, :]
    after = table[group + 1][1:2, :]
    edge_ref[0:1, :] = before[:, :DH]
    edge_ref[1:2, :] = after[:, :DH]
    edge_ref[2:8, :] = jnp.zeros((6, DH), F32)
    norm = jnp.zeros((H, 256), F32)
    for k in range(1, group + 1):
        w = same(got_msg[k - 1, H : H + 1, :], before) * jnp.where(me >= k, 1.0, 0.0)
        norm = norm + w * got_msg[k - 1, 0:H, :]
    for h in range(H):
        nin_ref[h] = norm[h : h + 1, :]

    tokens = g_ref.shape[0]
    rows = row_docs(doc_ref, (tokens, 1), 0)
    inside = same(rows, before[:, :DH])
    head = same(rows, first)

    def adjoint_of(h, carry):
        columns = head_columns(h)
        feat = fq_ref[h].astype(F32)
        extra = jnp.sum(feat * nin_ref[h][:, :F], axis=1, keepdims=True)
        den = den0_ref[:, columns] + inside * extra
        den_ref[:, columns] = den
        high, low = halves(g_ref[:, columns].astype(F32) / den)
        both = dot((feat * head).astype(BF), jnp.concatenate([high, low], axis=1), (0, 0))
        adj[h] = both[:, :DH] + both[:, DH:]
        return carry

    for c in range(chunks):
        lax.fori_loop(c * CHUNK, (c + 1) * CHUNK, adjoint_of, 0)
        start(1, c, 0)

    weights = {}
    for kind in (0, 1):
        near = before if kind == 0 else after
        for r, b in enumerate(rounds):
            u = lax.rem(me // b, 2)
            own = (me // b) * b
            other = own + b - 2 * b * u
            shift = b - 1 if kind == 0 else 0
            far = doc_at(other + shift, kind)
            w = same(doc_at(own + shift, kind), far)[:, :DH]
            wp = same(far, near)[:, :DH]
            up = (u if kind == 0 else 1 - u).astype(F32)
            keep = up + (1.0 - up) * w
            weights[kind, r] = (up * wp, keep, 1.0 - up, up * w + (1.0 - up))
        base = (me // group) * group
        far = doc_at(base - 1 if kind == 0 else base + group, kind)
        weights[kind, last_round] = same(far, near)[:, :DH]

    def finish(kind, c, r):
        heads = pl.ds(c * CHUNK, CHUNK)
        result = s_ref if kind == 0 else a_ref
        copy = copy_of(kind, c, r)
        if r == last_round:
            @pl.when(can_down if kind == 0 else can_up)
            def _():
                copy.wait_recv()
                result[heads] = result[heads] + weights[kind, r] * got[kind, r, heads]
            return
        copy.wait_recv()
        wp, keep, take, add = weights[kind, r]

        def one(h, carry):
            came = got[kind, r, h]
            if r == 0:
                held = (state_ref if kind == 0 else adj)[h]
                result[h] = wp * came
                suffix[kind, h] = keep * held + take * came
            else:
                held = part[kind, r - 1, h]
                result[h] = result[h] + wp * came
                suffix[kind, h] = keep * suffix[kind, h] + take * came
            if r + 1 < last_round:
                part[kind, r, h] = keep * held + add * came
            return carry

        lax.fori_loop(c * CHUNK, (c + 1) * CHUNK, one, 0)
        start(kind, c, r + 1)

    items = [(kind, c) for kind in (0, 1) for c in range(chunks)]
    for wave in range(len(items) + last_round):
        for r in range(last_round, -1, -1):
            if 0 <= wave - r < len(items):
                finish(*items[wave - r], r)

    for copy in small:
        copy.wait_send()
    for kind, c in items:
        for r in range(last_round):
            copy_of(kind, c, r).wait_send()

        @pl.when(can_up if kind == 0 else can_down)
        def _():
            copy_of(kind, c, last_round).wait_send()


def backward_kernel(
    doc_ref, edge_ref, q_ref, k_ref, v_ref, g_ref, w_ref, fq_ref, probs_ref, s_ref, a_ref, nin_ref, den_ref,
    out_ref, qg_ref, vg_ref, gfk_ref, hn_ref, wg_ref,
):
    tokens = q_ref.shape[0]
    rows = row_docs(doc_ref, (tokens, 1), 0)
    columns = row_docs(doc_ref, (1, tokens), 1)
    mask = jnp.logical_and(
        lax.broadcasted_iota(jnp.int32, (tokens, tokens), 1)
        <= lax.broadcasted_iota(jnp.int32, (tokens, tokens), 0),
        rows == columns,
    )
    inside = same(rows, edge_ref[0:1, :])
    beyond = same(rows, edge_ref[1:2, :])
    inside_f = inside[:, 0:1]
    beyond_f = beyond[:, 0:1]
    head = same(rows, doc_ref[0, 0].astype(F32))
    weight = w_ref[...]
    total = jnp.zeros((DH, F), F32)
    for j in range(STEP):
        part = slice(j * DH, (j + 1) * DH)
        value = v_ref[:, part]
        grad = g_ref[:, part].astype(F32)
        feat_q = fq_ref[j]
        probs = probs_ref[j]
        den = den_ref[:, part]
        proj_q = dot(q_ref[:, part], weight, (1, 0))
        feat_k = features(dot(k_ref[:, part], weight, (1, 0)))
        s_high, s_low = halves(s_ref[j])
        a_high, a_low = halves(a_ref[j])
        carried = dot(feat_q, jnp.concatenate([s_high, s_low], axis=1), (1, 0))
        out = (dot(probs, value, (1, 0)) + inside * (carried[:, :DH] + carried[:, DH:])) / den
        out_ref[:, part] = out
        drift = -jnp.sum(grad * out, axis=1, keepdims=True) / den[:, 0:1]
        line = jnp.sum(feat_q.astype(F32) * (head * drift), axis=0, keepdims=True)
        hn_ref[j] = jnp.concatenate([line, jnp.zeros((1, 256 - F), F32)], axis=1)
        high, low = halves(grad / den)
        dprobs = jnp.where(mask, dot(high, value, (1, 1)) + drift, 0.0).astype(BF)
        cross = dot(
            jnp.concatenate([high, low, high], axis=1),
            jnp.concatenate([s_high, s_high, s_low], axis=1), (1, 1))
        grad_fq = dot(dprobs, feat_k, (1, 0)) + inside_f * (cross + nin_ref[j][:, :F] * drift)
        gfk_ref[j] = dot(dprobs, feat_q, (0, 0)) + beyond_f * dot(
            jnp.concatenate([value, value], axis=1), jnp.concatenate([a_high, a_low], axis=1), (1, 1))
        later = dot(feat_k, jnp.concatenate([a_high, a_low], axis=1), (1, 0))
        vg_ref[:, part] = dot(probs, high, (0, 0)) + beyond * (later[:, :DH] + later[:, DH:])
        grad_pq = (grad_fq * (1.0 + proj_q)).astype(BF)
        qg_ref[:, part] = dot(grad_pq, weight, (1, 1))
        total = total + dot(q_ref[:, part], grad_pq, (0, 0))

    @pl.when(pl.program_id(0) == 0)
    def _():
        wg_ref[...] = total

    @pl.when(pl.program_id(0) > 0)
    def _():
        wg_ref[...] = wg_ref[...] + total


def update_kernel(
    n, dp, group, doc_ref, hn_ref, gfk_ref, k_ref, w_ref, wg_ref,
    kg_ref, new_ref,
    msg, got_msg, drifts, held, got, ms, mr, send, recv,
):
    me = lax.axis_index("ctx")
    row = lax.axis_index("dp")
    hops = [("dp", b) for b in bits(dp)] + [("ctx", b) for b in bits(n)]

    def partner(axis, b):
        at = row if axis == "dp" else me
        return {axis: at + b - 2 * b * lax.rem(at // b, 2)}

    barrier = pltpu.get_barrier_semaphore()
    greeted = 2 * group
    for k in range(1, group + 1):
        for target in (lax.rem(me + k, n), lax.rem(me + n - k, n)):
            pl.semaphore_signal(barrier, inc=1, device_id={"ctx": target}, device_id_type=MESH)
    for axis, b in hops:
        if axis == "dp" or b > group:
            greeted += 1
            pl.semaphore_signal(barrier, inc=1, device_id=partner(axis, b), device_id_type=MESH)

    first = doc_ref[0, 0].astype(F32)
    for h in range(H):
        msg[h : h + 1, :] = hn_ref[h]
    msg[H : H + 8, :] = jnp.broadcast_to(first, (8, 256))
    pl.semaphore_wait(barrier, greeted)
    small = []
    for k in range(1, group + 1):
        small.append(pltpu.make_async_remote_copy(
            src_ref=msg, dst_ref=got_msg.at[k - 1], send_sem=ms.at[k - 1], recv_sem=mr.at[k - 1],
            device_id={"ctx": lax.rem(me + n - k, n)}, device_id_type=MESH))
    for copy in small:
        copy.start()
    for copy in small:
        copy.wait_recv()
    near = got_msg[0, H : H + 1, :]
    norm = jnp.zeros((H, 256), F32)
    for k in range(1, group + 1):
        w = same(got_msg[k - 1, H : H + 1, :], near) * jnp.where(me + k < n, 1.0, 0.0)
        norm = norm + w * got_msg[k - 1, 0:H, :]
    for h in range(H):
        drifts[h] = norm[h : h + 1, :]
    tokens = k_ref.shape[0]
    beyond = same(row_docs(doc_ref, (tokens, 1), 0), near)[:, :F]
    weight = w_ref[...]

    def one(h, total):
        columns = head_columns(h)
        key = k_ref[:, columns]
        grad_fk = gfk_ref[h] + beyond * drifts[h][:, :F]
        grad_pk = (grad_fk * (1.0 + dot(key, weight, (1, 0)))).astype(BF)
        kg_ref[:, columns] = dot(grad_pk, weight, (1, 1))
        return total + dot(key, grad_pk, (0, 0))

    total = lax.fori_loop(0, H, one, wg_ref[...])
    copies = []
    for r, (axis, b) in enumerate(hops):
        held[r] = total
        copy = pltpu.make_async_remote_copy(
            src_ref=held.at[r], dst_ref=got.at[r], send_sem=send.at[r], recv_sem=recv.at[r],
            device_id=partner(axis, b), device_id_type=MESH)
        copy.start()
        copy.wait_recv()
        copies.append(copy)
        total = total + got[r]
    scale = lax.rsqrt(jnp.sum(total * total, keepdims=True) / (DH * F) + EPSILON)
    new_ref[...] = weight.astype(F32) - RATE * total * scale
    for copy in small + copies:
        copy.wait_send()


def shards(n, dp, queries, keys, values, doc_ids, feat_weight, out_grad):
    tokens = queries.shape[1]
    wide = H * DH
    group = max(1, n // 4)
    q, k, v, g = (x.reshape(tokens, wide) for x in (queries, keys, values, out_grad))
    shape = jax.ShapeDtypeStruct
    smem = pl.BlockSpec(memory_space=pltpu.SMEM)
    vmem = pl.BlockSpec(memory_space=pltpu.VMEM)
    cols = pl.BlockSpec((tokens, STEP * DH), lambda i: (0, i))
    whole = pl.BlockSpec((DH, F), lambda i: (0, 0))

    def per_head(*dims):
        return pl.BlockSpec((STEP,) + dims, lambda i: (i, 0, 0))

    feat_q, probs, state, norm, den0 = pl.pallas_call(
        local_kernel,
        grid=(H // STEP,),
        in_specs=[smem, cols, cols, cols, whole],
        out_specs=[per_head(tokens, F), per_head(tokens, tokens), per_head(F, DH), per_head(1, 256), cols],
        out_shape=[
            shape((H, tokens, F), BF), shape((H, tokens, tokens), BF), shape((H, F, DH), F32),
            shape((H, 1, 256), F32), shape((tokens, wide), F32),
        ],
        compiler_params=pltpu.CompilerParams(vmem_limit_bytes=LIMIT),
    )(doc_ids, q, k, v, feat_weight)

    rounds = len(bits(group))
    slots = 2 * (H // CHUNK) * (rounds + 1)
    dma = pltpu.SemaphoreType.DMA
    state_in, adjoint, norm_in, den, edge = pl.pallas_call(
        functools.partial(exchange_kernel, n, group),
        in_specs=[smem] + [vmem] * 5,
        out_specs=[vmem] * 5,
        out_shape=[
            shape((H, F, DH), F32), shape((H, F, DH), F32), shape((H, 1, 256), F32),
            shape((tokens, wide), F32), shape((8, DH), F32),
        ],
        scratch_shapes=[
            pltpu.VMEM((H + 8, 256), F32),
            pltpu.VMEM((8, 256), F32),
            pltpu.VMEM((2 * group + 1, 8, 256), F32),
            pltpu.VMEM((group, H + 8, 256), F32),
            pltpu.VMEM((group, 8, 256), F32),
            pltpu.VMEM((H, F, DH), F32),
            pltpu.VMEM((2, max(1, rounds - 1), H, F, DH), F32),
            pltpu.VMEM((2, H, F, DH), F32),
            pltpu.VMEM((2, rounds + 1, H, F, DH), F32),
            dma((group,)), dma((group,)), dma((group,)), dma((group,)), dma((slots,)), dma((slots,)),
        ],
        compiler_params=pltpu.CompilerParams(
            collective_id=0, has_side_effects=True, vmem_limit_bytes=LIMIT),
    )(doc_ids, feat_q, state, norm, den0, g)

    out, query_grad, value_grad, grad_fk, head_norm, weight_q = pl.pallas_call(
        backward_kernel,
        grid=(H // STEP,),
        in_specs=[
            smem, pl.BlockSpec((8, DH), lambda i: (0, 0)), cols, cols, cols, cols, whole,
            per_head(tokens, F), per_head(tokens, tokens), per_head(F, DH), per_head(F, DH),
            per_head(1, 256), cols,
        ],
        out_specs=[cols, cols, cols, per_head(tokens, F), per_head(1, 256), whole],
        out_shape=[shape((tokens, wide), F32)] * 3 + [
            shape((H, tokens, F), F32), shape((H, 1, 256), F32), shape((DH, F), F32)],
        compiler_params=pltpu.CompilerParams(vmem_limit_bytes=LIMIT),
    )(doc_ids, edge, q, k, v, g, feat_weight, feat_q, probs, state_in, adjoint, norm_in, den)

    steps = len(bits(n)) + len(bits(dp))
    key_grad, new_weight = pl.pallas_call(
        functools.partial(update_kernel, n, dp, group),
        in_specs=[smem] + [vmem] * 5,
        out_specs=[vmem] * 2,
        out_shape=[shape((tokens, wide), F32), shape((DH, F), F32)],
        scratch_shapes=[
            pltpu.VMEM((H + 8, 256), F32),
            pltpu.VMEM((group, H + 8, 256), F32),
            pltpu.VMEM((H, 1, 256), F32),
            pltpu.VMEM((steps, DH, F), F32),
            pltpu.VMEM((steps, DH, F), F32),
            dma((group,)), dma((group,)), dma((steps,)), dma((steps,)),
        ],
        compiler_params=pltpu.CompilerParams(
            collective_id=1, has_side_effects=True, vmem_limit_bytes=LIMIT),
    )(doc_ids, head_norm, grad_fk, k, feat_weight, weight_q)

    full = (1, tokens, wide)
    return (
        out.reshape(full), query_grad.reshape(full), key_grad.reshape(full), value_grad.reshape(full),
        new_weight,
    )


def solution(mesh):
    split = P("dp", "ctx", None)
    return jax.shard_map(
        functools.partial(shards, mesh.shape["ctx"], mesh.shape["dp"]),
        mesh=mesh,
        in_specs=(split, split, split, P("dp", "ctx"), P(), split),
        out_specs=(split, split, split, split, P()),
        check_vma=False,
    )
```

time: 580 us -> 155 us (0.27)
  waiting for transfers between devices: 312 us -> 0 us
  Pallas kernels: 0 us -> 149 us
  starting transfers between devices: 126 us -> 0 us
  other arithmetic: 36.5 us -> 0 us
  between operations: 35.9 us -> 0.66 us
  matrix products: 30.7 us -> 0 us
  local copies, waits for them, and re-layouts: 35.8 us -> 5.45 us
    ppermute x20 -> x0, waiting for transfers between devices: 188 us -> none  [passed_along(): return lax.ppermute(array, axis, pairs)]
    pallas_call x0 -> x4, Pallas kernels: none -> 149 us  [the longest x1 89.7 us: shards(): pl.pallas_call(functools.partial(exchange_kernel, n, group), in_specs=[sm...]
    ppermute x20 -> x0, starting transfers between devices: 126 us -> none  [passed_along(): return lax.ppermute(array, axis, pairs)]
    psum x1 -> x0, waiting for transfers between devices: 124 us -> none  [shards(): weight_grad = lax.psum(weight_part, ('dp', 'ctx'))]
    dot_general x21 -> x0, matrix products: 30.7 us -> none  [the longest x1 3.52 us: shards(): head_state = jnp.einsum('thf,thd->hfd', head_feat, scaled, precision=HIGH)]
    slice x38 -> x0, local copies, waits for them, and re-layouts: 20.8 us -> none  [the longest x16 9.59 us: chain_combine(): joined = later[0] == earlier[0]]
    select_n x18 -> x0, other arithmetic: 14.4 us -> none  [the longest x15 14.2 us: prefix(): total = jnp.where(valid(step), chain_combine(got, total), total)]
    add x17 -> x0, other arithmetic: 9.39 us -> none  [the longest x16 9.38 us: chain_combine(): later[1:] + jnp.where(joined, earlier[1:], jnp.zeros_like(earlier[1:]))]
  transfers between devices with their start and end apart: 21 -> 0, of which waited for: 15 -> 0; matrix products, arithmetic and copies ran while one was open for 11% -> 0% of each run, Pallas kernels for 0% -> 0%
where the time goes in v1:
time: 155 us
  Pallas kernels  149 us (96%)
  local copies, waits for them, and re-layouts  5.45 us (4%)
    pallas_call x1, Pallas kernels, shards(): pl.pallas_call(functools.partial(exchange_kernel, n, group), in_specs=[sm...  89.7 us
    pallas_call x1, Pallas kernels, shards(): pl.pallas_call(functools.partial(update_kernel, n, dp, group), in_specs=[...  37.6 us
    pallas_call x1, Pallas kernels, shards(): pl.pallas_call(backward_kernel, grid=(H // STEP,), in_specs=[smem, pl.Blo...  13.4 us
    pallas_call x1, Pallas kernels, shards(): pl.pallas_call(local_kernel, grid=(H // STEP,), in_specs=[smem, cols, col...  8.02 us
    unnamed x3, local copies, waits for them, and re-layouts  5.45 us

profile of v1, /device:TPU:0, one launch (start us, length us, event | category | flops | bytes accessed | tf_op | source)
XLA Modules:
  0.0 154.9 jit_solution(11062474038035829908)
XLA Ops:
  0.6 1.5 copy.11.w_ref
  2.1 8.0 %shard_map.101 = (bf16[16,128,160]{2,1,0:T(8,128)(2,1)}, bf16[16,128,128]{2,1,0:T(8,128)(2,1)}, f32[16,160,128]{2,1,0:T(8,128)}, f32[16,1,256]{2,1,0:T(1,128)}, f32[128,2048]{1,0:T(8,128)}) custom-call(s32[1,2]{1,0:T(1,128)} %doc_ref.7, bf16[128,2048]{1,0:T(8,128)(2,1)} %bitcast.13, bf16[128,2048]{1,0:T(8,128)(2,1)} %bitcast.8, bf16[128,2048]{1,0:T(8,128)(2,1)} %bitcast.15, ...), custom_call_target="tpu_custom_call" | custom-call | tf_op jit(solution)/shard_map/pallas_call | solution.py:408
  10.2 89.7 %shard_map.102 = (f32[16,160,128]{2,1,0:T(8,128)}, f32[16,160,128]{2,1,0:T(8,128)}, f32[16,1,256]{2,1,0:T(1,128)}, f32[128,2048]{1,0:T(8,128)}, f32[8,128]{1,0:T(8,128)}) custom-call(s32[1,2]{1,0:T(1,128)} %doc_ref.7, bf16[16,128,160]{2,1,0:T(8,128)(2,1)} %get-tuple-element.23.fq_ref, f32[16,160,128]{2,1,0:T(8,128)} %get-tuple-element.24.state_ref, ...), custom_call_target="tpu_custom_call" | custom-call | tf_op jit(solution)/shard_map/pallas_call | solution.py:423
  99.9 13.4 %shard_map.103 = (f32[128,2048]{1,0:T(8,128)}, f32[128,2048]{1,0:T(8,128)}, f32[128,2048]{1,0:T(8,128)}, f32[16,128,160]{2,1,0:T(8,128)}, f32[16,1,256]{2,1,0:T(1,128)}, /*index=5*/f32[128,160]{1,0:T(8,128)}) custom-call(s32[1,2]{1,0:T(1,128)} %doc_ref.7, f32[8,128]{1,0:T(8,128)} %get-tuple-element.27.edge_ref, bf16[128,2048]{1,0:T(8,128)(2,1)} %bitcast.14, ...), custom_call_target="tpu_custom_call" | custom-call | tf_op jit(solution)/shard_map/pallas_call | solution.py:447
  113.3 37.6 %shard_map.104 = (f32[128,2048]{1,0:T(8,128)}, f32[128,160]{1,0:T(8,128)}) custom-call(s32[1,2]{1,0:T(1,128)} %doc_ref.7, f32[16,1,256]{2,1,0:T(1,128)} %get-tuple-element.35.hn_ref, f32[16,128,160]{2,1,0:T(8,128)} %get-tuple-element.36.gfk_ref, bf16[128,2048]{1,0:T(8,128)(2,1)} %bitcast.10, bf16[128,160]{1,0:T(8,128)(2,1)} %copy.11.w_ref, ...), custom_call_target="tpu_custom_call" | custom-call | tf_op jit(solution)/shard_map/pallas_call | solution.py:462
  151.0 1.6 %copy.14 = f32[128,160]{0,1:T(8,128)} copy(f32[128,160]{1,0:T(8,128)} %get-tuple-element.45) | data formatting | bytes 163840
  152.6 2.3 %copy.16 = f32[1,128,2048]{2,1,0:T(8,128)} copy(f32[1,128,2048]{2,1,0:T(8,128)} %bitcast.17) | data formatting | bytes 2097152

commit v2 on v1

v2 whole, which is shorter than its diff:
```python
import functools

import jax
import jax.numpy as jnp
from jax import lax
from jax.experimental import pallas as pl
from jax.experimental.pallas import tpu as pltpu
from jax.sharding import PartitionSpec as P

H = 16
DH = 128
F = 160
BLOCK = 64
RATE = 0.5
EPSILON = 1e-06
CHUNK = 2
LAG = 2
MESH = pl.DeviceIdType.MESH
BF = jnp.bfloat16
F32 = jnp.float32
LIMIT = 56 * 1024 * 1024


def dot(a, b, dims):
    return lax.dot_general(a, b, ((dims[:1], dims[1:]), ((), ())), preferred_element_type=F32)


def features(proj):
    return (1.0 + proj + 0.5 * proj * proj).astype(BF)


def halves(x):
    high = x.astype(BF)
    return high, (x - high.astype(F32)).astype(BF)


def row_docs(doc_ref, shape, dim):
    place = lax.broadcasted_iota(jnp.int32, shape, dim) // BLOCK
    docs = jnp.zeros(shape, F32)
    for block in range(doc_ref.shape[1]):
        docs = jnp.where(place == block, doc_ref[0, block].astype(F32), docs)
    return docs


def same(a, b):
    return jnp.where(a == b, 1.0, 0.0)


def bits(count):
    return [1 << r for r in range(count.bit_length() - 1)]


def kernel(
    n, dp, group, doc_ref, q_ref, k_ref, v_ref, g_ref, w_ref,
    out_ref, qg_ref, kg_ref, vg_ref, new_ref,
    fq, fk, probs_s, den_s, s_s, a_s, nin_s, hn_s, drift_s,
    msg, note, table, got_msg, got_note, hmsg, got_hmsg,
    own_sum, part, suffix, got, acc, held, got_w, got_half, got_final,
    ms, mr, ns, nr, hs, hr, send, recv, wsend, wrecv,
):
    me = lax.axis_index("ctx")
    row = lax.axis_index("dp")
    tokens = q_ref.shape[0]
    rounds = bits(group)
    last_round = len(rounds)
    chunks = H // CHUNK
    hops = bits(n)

    def partner(b):
        return {"ctx": me + b - 2 * b * lax.rem(me // b, 2)}

    other_core = {"dp": 1 - row}

    barrier = pltpu.get_barrier_semaphore()
    greeted = 2 * group + 1
    for k in range(1, group + 1):
        for target in (lax.rem(me + k, n), lax.rem(me + n - k, n)):
            pl.semaphore_signal(barrier, inc=1, device_id={"ctx": target}, device_id_type=MESH)
    pl.semaphore_signal(barrier, inc=1, device_id=other_core, device_id_type=MESH)
    for b in hops:
        if b > group:
            greeted += 1
            pl.semaphore_signal(barrier, inc=1, device_id=partner(b), device_id_type=MESH)

    last = doc_ref[0, doc_ref.shape[1] - 1].astype(F32)
    first = doc_ref[0, 0].astype(F32)
    which = lax.broadcasted_iota(jnp.int32, (8, 256), 0)
    tile = jnp.where(which == 0, last, jnp.where(which == 1, first, 0.0))
    note[...] = tile
    table[group] = tile
    msg[H : H + 8, :] = tile
    hmsg[H : H + 8, :] = tile
    rows = row_docs(doc_ref, (tokens, 1), 0)
    mask = jnp.logical_and(
        lax.broadcasted_iota(jnp.int32, (tokens, tokens), 1)
        <= lax.broadcasted_iota(jnp.int32, (tokens, tokens), 0),
        rows == row_docs(doc_ref, (1, tokens), 1),
    )
    tail = same(rows, last)
    head = same(rows, first)
    weight = w_ref[...]
    ones = jnp.ones((tokens, DH), BF)
    zeros = jnp.zeros((1, 256 - F), F32)

    def heads_of(c):
        return range(c * CHUNK, (c + 1) * CHUNK)

    def columns(h):
        return slice(h * DH, (h + 1) * DH)

    def copy_of(kind, c, r):
        heads = pl.ds(c * CHUNK, CHUNK)
        if r < last_round:
            target = partner(rounds[r])
        else:
            target = {"ctx": me + group if kind == 0 else me - group}
        if r == 0:
            source = own_sum.at[kind, heads]
        elif r < last_round:
            source = part.at[kind, r - 1, heads]
        else:
            source = suffix.at[kind, heads]
        slot = (kind * chunks + c) * (last_round + 1) + r
        return pltpu.make_async_remote_copy(
            src_ref=source, dst_ref=got.at[kind, r, heads], send_sem=send.at[slot], recv_sem=recv.at[slot],
            device_id=target, device_id_type=MESH)

    can_up = me + group < n
    can_down = me >= group

    def start(kind, c, r):
        if r < last_round:
            copy_of(kind, c, r).start()
        else:
            @pl.when(can_up if kind == 0 else can_down)
            def _():
                copy_of(kind, c, r).start()

    for c in range(chunks):
        for h in heads_of(c):
            feat = features(dot(k_ref[:, columns(h)], weight, (1, 0)))
            fk[h] = feat
            tail_k = feat.astype(F32) * tail
            own_sum[0, h] = dot(tail_k.astype(BF), v_ref[:, columns(h)], (0, 0))
            line = jnp.sum(tail_k, axis=0, keepdims=True)
            msg[h : h + 1, :] = jnp.concatenate([line, zeros], axis=1)
        if c == 0:
            pl.semaphore_wait(barrier, greeted)
        start(0, c, 0)

    small = []
    for k in range(1, group + 1):
        small.append(pltpu.make_async_remote_copy(
            src_ref=msg, dst_ref=got_msg.at[k - 1], send_sem=ms.at[k - 1], recv_sem=mr.at[k - 1],
            device_id={"ctx": lax.rem(me + k, n)}, device_id_type=MESH))
        small.append(pltpu.make_async_remote_copy(
            src_ref=note, dst_ref=got_note.at[k - 1], send_sem=ns.at[k - 1], recv_sem=nr.at[k - 1],
            device_id={"ctx": lax.rem(me + n - k, n)}, device_id_type=MESH))
    for copy in small:
        copy.start()

    def scores(c):
        for h in heads_of(c):
            feat_q = features(dot(q_ref[:, columns(h)], weight, (1, 0)))
            probs = jnp.where(mask, dot(feat_q, fk[h], (1, 1)), 0.0).astype(BF)
            fq[h] = feat_q
            probs_s[h] = probs
            den_s[:, columns(h)] = dot(probs, ones, (1, 0))

    scores(0)
    scores(1)
    for copy in small:
        copy.wait_recv()
    for k in range(1, group + 1):
        table[group - k] = got_msg[k - 1, H : H + 8, :]
        table[group + k] = got_note[k - 1]

    def doc_at(index, kind):
        return table[index - me + group][kind : kind + 1, :]

    before = table[group - 1][0:1, :]
    after = table[group + 1][1:2, :]
    norm = jnp.zeros((H, 256), F32)
    for k in range(1, group + 1):
        w = same(got_msg[k - 1, H : H + 1, :], before) * jnp.where(me >= k, 1.0, 0.0)
        norm = norm + w * got_msg[k - 1, 0:H, :]
    nin_s[...] = norm
    inside = same(rows, before[:, :DH])
    beyond = same(rows, after[:, :DH])
    inside_f = inside[:, 0:1]
    beyond_f = beyond[:, 0:1]

    def adjoint(c):
        for h in heads_of(c):
            feat = fq[h].astype(F32)
            extra = jnp.sum(feat * nin_s[h : h + 1, :F], axis=1, keepdims=True)
            den = den_s[:, columns(h)] + inside * extra
            den_s[:, columns(h)] = den
            high, low = halves(g_ref[:, columns(h)].astype(F32) / den)
            both = dot((feat * head).astype(BF), jnp.concatenate([high, low], axis=1), (0, 0))
            own_sum[1, h] = both[:, :DH] + both[:, DH:]

    weights = {}
    for kind in (0, 1):
        near = before if kind == 0 else after
        for r, b in enumerate(rounds):
            u = lax.rem(me // b, 2)
            own = (me // b) * b
            other = own + b - 2 * b * u
            shift = b - 1 if kind == 0 else 0
            far = doc_at(other + shift, kind)
            w = same(doc_at(own + shift, kind), far)[:, :DH]
            wp = same(far, near)[:, :DH]
            up = (u if kind == 0 else 1 - u).astype(F32)
            keep = up + (1.0 - up) * w
            weights[kind, r] = (up * wp, keep, 1.0 - up, up * w + (1.0 - up))
        base = (me // group) * group
        far = doc_at(base - 1 if kind == 0 else base + group, kind)
        weights[kind, last_round] = same(far, near)[:, :DH]

    def finish(kind, c, r):
        heads = pl.ds(c * CHUNK, CHUNK)
        result = s_s if kind == 0 else a_s
        copy = copy_of(kind, c, r)
        if r == last_round:
            @pl.when(can_down if kind == 0 else can_up)
            def _():
                copy.wait_recv()
                result[heads] = result[heads] + weights[kind, r] * got[kind, r, heads]
            return
        copy.wait_recv()
        wp, keep, take, add = weights[kind, r]
        for h in heads_of(c):
            came = got[kind, r, h]
            if r == 0:
                mine = own_sum[kind, h]
                result[h] = wp * came
                suffix[kind, h] = keep * mine + take * came
            else:
                mine = part[kind, r - 1, h]
                result[h] = result[h] + wp * came
                suffix[kind, h] = keep * suffix[kind, h] + take * came
            if r + 1 < last_round:
                part[kind, r, h] = keep * mine + add * came
        start(kind, c, r + 1)

    def query_side(c, total):
        for h in heads_of(c):
            grad = g_ref[:, columns(h)].astype(F32)
            feat_q = fq[h]
            den = den_s[:, columns(h)]
            value = v_ref[:, columns(h)]
            query = q_ref[:, columns(h)]
            s_high, s_low = halves(s_s[h])
            carried = dot(feat_q, jnp.concatenate([s_high, s_low], axis=1), (1, 0))
            out = (dot(probs_s[h], value, (1, 0)) + inside * (carried[:, :DH] + carried[:, DH:])) / den
            out_ref[:, columns(h)] = out
            drift = -jnp.sum(grad * out, axis=1, keepdims=True) / den[:, 0:1]
            line = jnp.sum(feat_q.astype(F32) * (head * drift), axis=0, keepdims=True)
            hmsg[h : h + 1, :] = jnp.concatenate([line, zeros], axis=1)
            high, low = halves(grad / den)
            dprobs = jnp.where(mask, dot(high, value, (1, 1)) + drift, 0.0).astype(BF)
            cross = dot(
                jnp.concatenate([high, low, high], axis=1),
                jnp.concatenate([s_high, s_high, s_low], axis=1), (1, 1))
            grad_fq = dot(dprobs, fk[h], (1, 0)) + inside_f * (cross + nin_s[h : h + 1, :F] * drift)
            hn_s[h] = dot(dprobs, feat_q, (0, 0))
            vg_ref[:, columns(h)] = dot(probs_s[h], high, (0, 0))
            grad_pq = (grad_fq * (1.0 + dot(query, weight, (1, 0)))).astype(BF)
            qg_ref[:, columns(h)] = dot(grad_pq, weight, (1, 1))
            total = total + dot(grad_pq, query, (0, 0))
        return total

    def key_side(c, total):
        for h in heads_of(c):
            value = v_ref[:, columns(h)]
            key = k_ref[:, columns(h)]
            split = jnp.concatenate(halves(a_s[h]), axis=1)
            later = dot(fk[h], split, (1, 0))
            vg_ref[:, columns(h)] = vg_ref[:, columns(h)] + beyond * (later[:, :DH] + later[:, DH:])
            from_later = dot(jnp.concatenate([value, value], axis=1), split, (1, 1))
            grad_fk = hn_s[h] + beyond_f * (from_later + drift_s[h : h + 1, :F])
            grad_pk = (grad_fk * (1.0 + dot(key, weight, (1, 0)))).astype(BF)
            kg_ref[:, columns(h)] = dot(grad_pk, weight, (1, 1))
            total = total + dot(grad_pk, key, (0, 0))
        return total

    drifts = []
    for k in range(1, group + 1):
        drifts.append(pltpu.make_async_remote_copy(
            src_ref=hmsg, dst_ref=got_hmsg.at[k - 1], send_sem=hs.at[k - 1], recv_sem=hr.at[k - 1],
            device_id={"ctx": lax.rem(me + n - k, n)}, device_id_type=MESH))

    def take_drifts():
        for copy in drifts:
            copy.wait_recv()
        norm = jnp.zeros((H, 256), F32)
        for k in range(1, group + 1):
            w = same(got_hmsg[k - 1, H + 1 : H + 2, :], after) * jnp.where(me + k < n, 1.0, 0.0)
            norm = norm + w * got_hmsg[k - 1, 0:H, :]
        drift_s[...] = norm

    items = [(kind, c) for kind in (0, 1) for c in range(chunks)]
    drain = LAG * last_round
    key_from = chunks + drain + 1
    total = jnp.zeros((F, DH), F32)
    keys_done = 0
    for wave in range(len(items) + drain):
        for r in range(last_round + 1):
            if 0 <= wave - LAG * r < len(items):
                finish(*items[wave - LAG * r], r)
        if wave < chunks:
            if 2 <= wave + 2 < chunks:
                scores(wave + 2)
            adjoint(wave)
            start(1, wave, 0)
        if 0 <= wave - drain < chunks:
            total = query_side(wave - drain, total)
        if wave - drain == chunks - 1:
            for copy in drifts:
                copy.start()
        if wave == key_from:
            take_drifts()
        if wave >= key_from:
            while keys_done <= wave - drain - chunks and keys_done < chunks:
                total = key_side(keys_done, total)
                keys_done += 1
    assert keys_done == chunks

    half = F // dp
    acc[...] = total
    mine = pl.ds(row * half, half)
    theirs = pl.ds((1 - row) * half, half)
    sums = [pltpu.make_async_remote_copy(
        src_ref=acc.at[theirs], dst_ref=got_half, send_sem=wsend.at[0], recv_sem=wrecv.at[0],
        device_id=other_core, device_id_type=MESH)]
    sums[0].start()
    sums[0].wait_recv()
    total = acc[mine] + got_half[...]
    for r, b in enumerate(hops):
        held[r] = total
        copy = pltpu.make_async_remote_copy(
            src_ref=held.at[r], dst_ref=got_w.at[r], send_sem=wsend.at[r + 1], recv_sem=wrecv.at[r + 1],
            device_id=partner(b), device_id_type=MESH)
        copy.start()
        copy.wait_recv()
        sums.append(copy)
        total = total + got_w[r]
    steps = len(hops)
    held[steps] = total
    copy = pltpu.make_async_remote_copy(
        src_ref=held.at[steps], dst_ref=got_final, send_sem=wsend.at[steps + 1], recv_sem=wrecv.at[steps + 1],
        device_id=other_core, device_id_type=MESH)
    copy.start()
    sums.append(copy)
    copy.wait_recv()
    for copy in sums:
        copy.wait_send()
    acc[mine] = total
    acc[theirs] = got_final[...]
    whole = acc[...]
    scale = lax.rsqrt(jnp.sum(whole * whole, keepdims=True) / (DH * F) + EPSILON)
    new_ref[...] = weight.astype(F32) - jnp.transpose(RATE * whole * scale)

    for copy in small + drifts:
        copy.wait_send()
    for kind, c in items:
        for r in range(last_round):
            copy_of(kind, c, r).wait_send()

        @pl.when(can_up if kind == 0 else can_down)
        def _():
            copy_of(kind, c, last_round).wait_send()


def shards(n, dp, queries, keys, values, doc_ids, feat_weight, out_grad):
    tokens = queries.shape[1]
    wide = H * DH
    group = max(2, n // 4)
    q, k, v, g = (x.reshape(tokens, wide) for x in (queries, keys, values, out_grad))
    rounds = len(bits(group))
    steps = len(bits(n))
    slots = 2 * (H // CHUNK) * (rounds + 1)
    shape = jax.ShapeDtypeStruct
    vmem = pl.BlockSpec(memory_space=pltpu.VMEM)
    dma = pltpu.SemaphoreType.DMA
    results = pl.pallas_call(
        functools.partial(kernel, n, dp, group),
        in_specs=[pl.BlockSpec(memory_space=pltpu.SMEM)] + [vmem] * 5,
        out_specs=[vmem] * 5,
        out_shape=[shape((tokens, wide), F32)] * 4 + [shape((DH, F), F32)],
        scratch_shapes=[
            pltpu.VMEM((H, tokens, F), BF),
            pltpu.VMEM((H, tokens, F), BF),
            pltpu.VMEM((H, tokens, tokens), BF),
            pltpu.VMEM((tokens, wide), F32),
            pltpu.VMEM((H, F, DH), F32),
            pltpu.VMEM((H, F, DH), F32),
            pltpu.VMEM((H, 256), F32),
            pltpu.VMEM((H, tokens, F), F32),
            pltpu.VMEM((H, 256), F32),
            pltpu.VMEM((H + 8, 256), F32),
            pltpu.VMEM((8, 256), F32),
            pltpu.VMEM((2 * group + 1, 8, 256), F32),
            pltpu.VMEM((group, H + 8, 256), F32),
            pltpu.VMEM((group, 8, 256), F32),
            pltpu.VMEM((H + 8, 256), F32),
            pltpu.VMEM((group, H + 8, 256), F32),
            pltpu.VMEM((2, H, F, DH), F32),
            pltpu.VMEM((2, max(1, rounds - 1), H, F, DH), F32),
            pltpu.VMEM((2, H, F, DH), F32),
            pltpu.VMEM((2, rounds + 1, H, F, DH), F32),
            pltpu.VMEM((F, DH), F32),
            pltpu.VMEM((steps + 1, F // dp, DH), F32),
            pltpu.VMEM((steps, F // dp, DH), F32),
            pltpu.VMEM((F // dp, DH), F32),
            pltpu.VMEM((F // dp, DH), F32),
            dma((group,)), dma((group,)), dma((group,)), dma((group,)), dma((group,)), dma((group,)),
            dma((slots,)), dma((slots,)), dma((steps + 2,)), dma((steps + 2,)),
        ],
        compiler_params=pltpu.CompilerParams(
            collective_id=0, has_side_effects=True, vmem_limit_bytes=LIMIT),
    )(doc_ids, q, k, v, g, feat_weight)
    full = (1, tokens, wide)
    return tuple(x.reshape(full) for x in results[:4]) + (results[4],)


def solution(mesh):
    split = P("dp", "ctx", None)
    return jax.shard_map(
        functools.partial(shards, mesh.shape["ctx"], mesh.shape["dp"]),
        mesh=mesh,
        in_specs=(split, split, split, P("dp", "ctx"), P(), split),
        out_specs=(split, split, split, split, P()),
        check_vma=False,
    )
```

time: 155 us -> 128 us (0.83)
  Pallas kernels: 149 us -> 117 us
  local copies, waits for them, and re-layouts: 5.45 us -> 9.71 us
    pallas_call x4 -> x1, Pallas kernels: 149 us -> 117 us  [shards(): pl.pallas_call(functools.partial(kernel, n, dp, group), in_specs=[pl.Bloc...]
    unnamed x3 -> x12, local copies, waits for them, and re-layouts: 5.45 us -> 9.71 us
where the time goes in v2:
time: 128 us; the launch traced here: 127 us
  Pallas kernels  117 us (91%)
  local copies, waits for them, and re-layouts  9.71 us (8%)
    pallas_call x1, Pallas kernels, shards(): pl.pallas_call(functools.partial(kernel, n, dp, group), in_specs=[pl.Bloc...  117 us
    unnamed x12, local copies, waits for them, and re-layouts  9.71 us

profile of v2, /device:TPU:0, one launch (start us, length us, event | category | flops | bytes accessed | tf_op | source)
XLA Modules:
  0.0 127.2 jit_solution(3725071756609434037)
XLA Ops:
  0.6 1.5 %copy.11.w_ref = bf16[128,160]{1,0:T(8,128)(2,1)} copy(bf16[128,160]{0,1:T(8,128)(2,1)} %param.10) | data formatting | bytes 81920 | tf_op args[4]
  2.1 116.9 %shard_map.101 = (f32[128,2048]{1,0:T(8,128)}, f32[128,2048]{1,0:T(8,128)}, f32[128,2048]{1,0:T(8,128)}, f32[128,2048]{1,0:T(8,128)}, f32[128,160]{1,0:T(8,128)}) custom-call(s32[1,2]{1,0:T(1,128)} %doc_ref.1, bf16[128,2048]{1,0:T(8,128)(2,1)} %bitcast.12, bf16[128,2048]{1,0:T(8,128)(2,1)} %bitcast.13, bf16[128,2048]{1,0:T(8,128)(2,1)} %bitcast.14, ...), custom_call_target="tpu_custom_call" | custom-call | tf_op jit(solution)/shard_map/pallas_call | solution.py:387
  119.0 1.6 %copy.12 = f32[128,160]{0,1:T(8,128)} copy(f32[128,160]{1,0:T(8,128)} %get-tuple-element.19) | data formatting | bytes 163840
  120.7 0.0 copy-start.2
  120.7 2.4 %copy.17 = f32[1,128,2048]{2,1,0:T(8,128)} copy(f32[1,128,2048]{2,1,0:T(8,128)} %bitcast.11) | data formatting | bytes 2097152
  123.1 0.0 copy-done.2
  123.1 0.0 copy-start.1
  123.1 1.0 copy.18
  124.0 0.6 copy-done.1
  124.7 0.0 copy-start
  124.7 1.0 copy.19
  125.6 0.6 copy-done
  126.3 1.0 copy.20
Async XLA Ops:
  120.7 2.4 %copy-start.2 = (f32[128,2048]{1,0:T(8,128)S(1)}, f32[128,2048]{1,0:T(8,128)}, u32[]{:S(2)}) copy-start(f32[128,2048]{1,0:T(8,128)} %get-tuple-element.11) | copy-start | bytes 3145732
  123.1 1.6 %copy-start.1 = (f32[128,2048]{1,0:T(8,128)S(1)}, f32[128,2048]{1,0:T(8,128)}, u32[]{:S(2)}) copy-start(f32[128,2048]{1,0:T(8,128)} %get-tuple-element.12) | copy-start | bytes 3145732
  124.7 1.6 %copy-start = (f32[128,2048]{1,0:T(8,128)S(1)}, f32[128,2048]{1,0:T(8,128)}, u32[]{:S(2)}) copy-start(f32[128,2048]{1,0:T(8,128)} %get-tuple-element.13) | copy-start | bytes 3145732

commit v3 on v2

--- a/solution.py
+++ b/solution.py
@@ -15,6 +15,7 @@
 EPSILON = 1e-06
 CHUNK = 2
 LAG = 2
+AHEAD = 3
 MESH = pl.DeviceIdType.MESH
 BF = jnp.bfloat16
 F32 = jnp.float32
@@ -136,17 +137,12 @@
             def _():
                 copy_of(kind, c, r).start()
 
-    for c in range(chunks):
-        for h in heads_of(c):
-            feat = features(dot(k_ref[:, columns(h)], weight, (1, 0)))
-            fk[h] = feat
-            tail_k = feat.astype(F32) * tail
-            own_sum[0, h] = dot(tail_k.astype(BF), v_ref[:, columns(h)], (0, 0))
-            line = jnp.sum(tail_k, axis=0, keepdims=True)
-            msg[h : h + 1, :] = jnp.concatenate([line, zeros], axis=1)
-        if c == 0:
-            pl.semaphore_wait(barrier, greeted)
-        start(0, c, 0)
+    for h in range(H):
+        feat = features(dot(k_ref[:, columns(h)], weight, (1, 1)))
+        fk[h] = feat
+        line = jnp.sum(feat.astype(F32) * tail, axis=0, keepdims=True)
+        msg[h : h + 1, :] = jnp.concatenate([line, zeros], axis=1)
+    pl.semaphore_wait(barrier, greeted)
 
     small = []
     for k in range(1, group + 1):
@@ -158,10 +154,16 @@
             device_id={"ctx": lax.rem(me + n - k, n)}, device_id_type=MESH))
     for copy in small:
         copy.start()
+    for c in range(chunks):
+        for h in heads_of(c):
+            tail_k = (fk[h].astype(F32) * tail).astype(BF)
+            own_sum[0, h] = dot(tail_k, v_ref[:, columns(h)], (0, 0))
+        if c < AHEAD:
+            start(0, c, 0)
 
     def scores(c):
         for h in heads_of(c):
-            feat_q = features(dot(q_ref[:, columns(h)], weight, (1, 0)))
+            feat_q = features(dot(q_ref[:, columns(h)], weight, (1, 1)))
             probs = jnp.where(mask, dot(feat_q, fk[h], (1, 1)), 0.0).astype(BF)
             fq[h] = feat_q
             probs_s[h] = probs
@@ -266,22 +268,26 @@
             grad_fq = dot(dprobs, fk[h], (1, 0)) + inside_f * (cross + nin_s[h : h + 1, :F] * drift)
             hn_s[h] = dot(dprobs, feat_q, (0, 0))
             vg_ref[:, columns(h)] = dot(probs_s[h], high, (0, 0))
-            grad_pq = (grad_fq * (1.0 + dot(query, weight, (1, 0)))).astype(BF)
-            qg_ref[:, columns(h)] = dot(grad_pq, weight, (1, 1))
+            grad_pq = (grad_fq * (1.0 + dot(query, weight, (1, 1)))).astype(BF)
+            qg_ref[:, columns(h)] = dot(grad_pq, weight, (1, 0))
             total = total + dot(grad_pq, query, (0, 0))
         return total
 
-    def key_side(c, total):
+    def key_first(c):
         for h in heads_of(c):
             value = v_ref[:, columns(h)]
-            key = k_ref[:, columns(h)]
             split = jnp.concatenate(halves(a_s[h]), axis=1)
             later = dot(fk[h], split, (1, 0))
             vg_ref[:, columns(h)] = vg_ref[:, columns(h)] + beyond * (later[:, :DH] + later[:, DH:])
             from_later = dot(jnp.concatenate([value, value], axis=1), split, (1, 1))
-            grad_fk = hn_s[h] + beyond_f * (from_later + drift_s[h : h + 1, :F])
-            grad_pk = (grad_fk * (1.0 + dot(key, weight, (1, 0)))).astype(BF)
-            kg_ref[:, columns(h)] = dot(grad_pk, weight, (1, 1))
+            hn_s[h] = hn_s[h] + beyond_f * from_later
+
+    def key_side(c, total):
+        for h in heads_of(c):
+            key = k_ref[:, columns(h)]
+            grad_fk = hn_s[h] + beyond_f * drift_s[h : h + 1, :F]
+            grad_pk = (grad_fk * (1.0 + dot(key, weight, (1, 1)))).astype(BF)
+            kg_ref[:, columns(h)] = dot(grad_pk, weight, (1, 0))
             total = total + dot(grad_pk, key, (0, 0))
         return total
 
@@ -302,7 +308,7 @@
 
     items = [(kind, c) for kind in (0, 1) for c in range(chunks)]
     drain = LAG * last_round
-    key_from = chunks + drain + 1
+    key_from = chunks + drain + 3
     total = jnp.zeros((F, DH), F32)
     keys_done = 0
     for wave in range(len(items) + drain):
@@ -313,7 +319,8 @@
             if 2 <= wave + 2 < chunks:
                 scores(wave + 2)
             adjoint(wave)
-            start(1, wave, 0)
+        if wave + AHEAD < len(items):
+            start(*items[wave + AHEAD], 0)
         if 0 <= wave - drain < chunks:
             total = query_side(wave - drain, total)
         if wave - drain == chunks - 1:
@@ -321,11 +328,15 @@
                 copy.start()
         if wave == key_from:
             take_drifts()
+        if 0 <= wave - drain - chunks:
+            key_first(wave - drain - chunks)
         if wave >= key_from:
-            while keys_done <= wave - drain - chunks and keys_done < chunks:
-                total = key_side(keys_done, total)
-                keys_done += 1
-    assert keys_done == chunks
+            for _ in range(2):
+                if keys_done <= wave - drain - chunks:
+                    total = key_side(keys_done, total)
+                    keys_done += 1
+    for c in range(keys_done, chunks):
+        total = key_side(c, total)
 
     half = F // dp
     acc[...] = total
@@ -360,7 +371,7 @@
     acc[theirs] = got_final[...]
     whole = acc[...]
     scale = lax.rsqrt(jnp.sum(whole * whole, keepdims=True) / (DH * F) + EPSILON)
-    new_ref[...] = weight.astype(F32) - jnp.transpose(RATE * whole * scale)
+    new_ref[...] = weight.astype(F32) - RATE * whole * scale
 
     for copy in small + drifts:
         copy.wait_send()
@@ -371,6 +382,11 @@
         @pl.when(can_up if kind == 0 else can_down)
         def _():
             copy_of(kind, c, last_round).wait_send()
+
+
+def hand_on(*refs):
+    for source, target in zip(refs[:4], refs[4:]):
+        target[...] = source[...]
 
 
 def shards(n, dp, queries, keys, values, doc_ids, feat_weight, out_grad):
@@ -388,7 +404,7 @@
         functools.partial(kernel, n, dp, group),
         in_specs=[pl.BlockSpec(memory_space=pltpu.SMEM)] + [vmem] * 5,
         out_specs=[vmem] * 5,
-        out_shape=[shape((tokens, wide), F32)] * 4 + [shape((DH, F), F32)],
+        out_shape=[shape((tokens, wide), F32)] * 4 + [shape((F, DH), F32)],
         scratch_shapes=[
             pltpu.VMEM((H, tokens, F), BF),
             pltpu.VMEM((H, tokens, F), BF),
@@ -420,9 +436,18 @@
         ],
         compiler_params=pltpu.CompilerParams(
             collective_id=0, has_side_effects=True, vmem_limit_bytes=LIMIT),
-    )(doc_ids, q, k, v, g, feat_weight)
+    )(doc_ids, q, k, v, g, feat_weight.T)
+    cols = pl.BlockSpec((tokens, wide // 4), lambda i: (0, i))
+    placed = pl.pallas_call(
+        hand_on,
+        grid=(4,),
+        in_specs=[cols] * 4,
+        out_specs=[cols] * 4,
+        out_shape=[shape((tokens, wide), F32)] * 4,
+        compiler_params=pltpu.CompilerParams(vmem_limit_bytes=LIMIT),
+    )(*results[:4])
     full = (1, tokens, wide)
-    return tuple(x.reshape(full) for x in results[:4]) + (results[4],)
+    return tuple(x.reshape(full) for x in placed) + (results[4].T,)
 
 
 def solution(mesh):

time: 128 us -> 102 us (0.80)
  Pallas kernels: 117 us -> 99.3 us
  local copies, waits for them, and re-layouts: 9.71 us -> 0.64 us
    pallas_call x1, Pallas kernels: 117 us -> 94.6 us  [shards(): pl.pallas_call(functools.partial(kernel, n, dp, group), in_specs=[pl.Bloc...]
    unnamed x12 -> x3, local copies, waits for them, and re-layouts: 9.71 us -> 0.64 us
    pallas_call x0 -> x1, Pallas kernels: none -> 4.7 us  [shards(): pl.pallas_call(hand_on, grid=(4,), in_specs=[cols] * 4, out_specs=[cols]...]
where the time goes in v3:
time: 102 us; the launch traced here: 101 us
  Pallas kernels  99.3 us (97%)
    pallas_call x1, Pallas kernels, shards(): pl.pallas_call(functools.partial(kernel, n, dp, group), in_specs=[pl.Bloc...  94.6 us
    pallas_call x1, Pallas kernels, shards(): pl.pallas_call(hand_on, grid=(4,), in_specs=[cols] * 4, out_specs=[cols]...  4.7 us

profile of v3, /device:TPU:0, one launch (start us, length us, event | category | flops | bytes accessed | tf_op | source)
XLA Modules:
  0.0 100.6 jit_solution(14721425983615225384)
XLA Ops:
  0.6 94.6 %shard_map.101 = (f32[128,2048]{1,0:T(8,128)}, f32[128,2048]{1,0:T(8,128)}, f32[128,2048]{1,0:T(8,128)}, f32[128,2048]{1,0:T(8,128)}, f32[160,128]{1,0:T(8,128)}) custom-call(s32[1,2]{1,0:T(1,128)} %doc_ref.1, bf16[128,2048]{1,0:T(8,128)(2,1)} %bitcast.10, bf16[128,2048]{1,0:T(8,128)(2,1)} %bitcast.11, bf16[128,2048]{1,0:T(8,128)(2,1)} %bitcast.12, ...), custom_call_target="tpu_custom_call" | custom-call | tf_op jit(solution)/shard_map/pallas_call | solution.py:403
  95.3 0.0 copy-start
  95.3 4.7 %shard_map.102 = (f32[128,2048]{1,0:T(8,128)}, f32[128,2048]{1,0:T(8,128)}, f32[128,2048]{1,0:T(8,128)}, f32[128,2048]{1,0:T(8,128)}) custom-call(f32[128,2048]{1,0:T(8,128)} %get-tuple-element.14.refs_0_, f32[128,2048]{1,0:T(8,128)} %get-tuple-element.15.refs_1_, f32[128,2048]{1,0:T(8,128)} %get-tuple-element.16.refs_2_, f32[128,2048]{1,0:T(8,128)} %get-tuple-element.17.refs_3_), custom_call_target="tpu_custom_call" | custom-call | tf_op jit(solution)/shard_map/pallas_call | solution.py:441
  100.0 0.0 copy-done
  100.0 0.6 copy.12
Async XLA Ops:
  95.3 4.7 %copy-start = (f32[160,128]{1,0:T(8,128)S(1)}, f32[160,128]{1,0:T(8,128)}, u32[]{:S(2)}) copy-start(f32[160,128]{1,0:T(8,128)} %get-tuple-element.22) | copy-start | bytes 245764

commit v4 on v3

--- a/solution.py
+++ b/solution.py
@@ -30,11 +30,6 @@
     return (1.0 + proj + 0.5 * proj * proj).astype(BF)
 
 
-def halves(x):
-    high = x.astype(BF)
-    return high, (x - high.astype(F32)).astype(BF)
-
-
 def row_docs(doc_ref, shape, dim):
     place = lax.broadcasted_iota(jnp.int32, shape, dim) // BLOCK
     docs = jnp.zeros(shape, F32)
@@ -54,7 +49,7 @@
 def kernel(
     n, dp, group, doc_ref, q_ref, k_ref, v_ref, g_ref, w_ref,
     out_ref, qg_ref, kg_ref, vg_ref, new_ref,
-    fq, fk, probs_s, den_s, s_s, a_s, nin_s, hn_s, drift_s,
+    fq, fk, slope_q, slope_k, probs_s, scaled_s, den_s, s_s, a_s, nin_s, hn_s, drift_s,
     msg, note, table, got_msg, got_note, hmsg, got_hmsg,
     own_sum, part, suffix, got, acc, held, got_w, got_half, got_final,
     ms, mr, ns, nr, hs, hr, send, recv, wsend, wrecv,
@@ -138,7 +133,9 @@
                 copy_of(kind, c, r).start()
 
     for h in range(H):
-        feat = features(dot(k_ref[:, columns(h)], weight, (1, 1)))
+        proj = dot(k_ref[:, columns(h)], weight, (1, 1))
+        slope_k[h] = 1.0 + proj
+        feat = features(proj)
         fk[h] = feat
         line = jnp.sum(feat.astype(F32) * tail, axis=0, keepdims=True)
         msg[h : h + 1, :] = jnp.concatenate([line, zeros], axis=1)
@@ -163,7 +160,9 @@
 
     def scores(c):
         for h in heads_of(c):
-            feat_q = features(dot(q_ref[:, columns(h)], weight, (1, 1)))
+            proj = dot(q_ref[:, columns(h)], weight, (1, 1))
+            slope_q[h] = 1.0 + proj
+            feat_q = features(proj)
             probs = jnp.where(mask, dot(feat_q, fk[h], (1, 1)), 0.0).astype(BF)
             fq[h] = feat_q
             probs_s[h] = probs
@@ -198,9 +197,9 @@
             extra = jnp.sum(feat * nin_s[h : h + 1, :F], axis=1, keepdims=True)
             den = den_s[:, columns(h)] + inside * extra
             den_s[:, columns(h)] = den
-            high, low = halves(g_ref[:, columns(h)].astype(F32) / den)
-            both = dot((feat * head).astype(BF), jnp.concatenate([high, low], axis=1), (0, 0))
-            own_sum[1, h] = both[:, :DH] + both[:, DH:]
+            scaled = (g_ref[:, columns(h)].astype(F32) / den).astype(BF)
+            scaled_s[h] = scaled
+            own_sum[1, h] = dot((feat * head).astype(BF), scaled, (0, 0))
 
     weights = {}
     for kind in (0, 1):
@@ -253,22 +252,20 @@
             den = den_s[:, columns(h)]
             value = v_ref[:, columns(h)]
             query = q_ref[:, columns(h)]
-            s_high, s_low = halves(s_s[h])
-            carried = dot(feat_q, jnp.concatenate([s_high, s_low], axis=1), (1, 0))
-            out = (dot(probs_s[h], value, (1, 0)) + inside * (carried[:, :DH] + carried[:, DH:])) / den
+            state = s_s[h].astype(BF)
+            carried = dot(feat_q, state, (1, 0))
+            out = (dot(probs_s[h], value, (1, 0)) + inside * carried) / den
             out_ref[:, columns(h)] = out
             drift = -jnp.sum(grad * out, axis=1, keepdims=True) / den[:, 0:1]
             line = jnp.sum(feat_q.astype(F32) * (head * drift), axis=0, keepdims=True)
             hmsg[h : h + 1, :] = jnp.concatenate([line, zeros], axis=1)
-            high, low = halves(grad / den)
+            high = scaled_s[h]
             dprobs = jnp.where(mask, dot(high, value, (1, 1)) + drift, 0.0).astype(BF)
-            cross = dot(
-                jnp.concatenate([high, low, high], axis=1),
-                jnp.concatenate([s_high, s_high, s_low], axis=1), (1, 1))
+            cross = dot(high, state, (1, 1))
             grad_fq = dot(dprobs, fk[h], (1, 0)) + inside_f * (cross + nin_s[h : h + 1, :F] * drift)
             hn_s[h] = dot(dprobs, feat_q, (0, 0))
             vg_ref[:, columns(h)] = dot(probs_s[h], high, (0, 0))
-            grad_pq = (grad_fq * (1.0 + dot(query, weight, (1, 1)))).astype(BF)
+            grad_pq = (grad_fq * slope_q[h]).astype(BF)
             qg_ref[:, columns(h)] = dot(grad_pq, weight, (1, 0))
             total = total + dot(grad_pq, query, (0, 0))
         return total
@@ -276,17 +273,17 @@
     def key_first(c):
         for h in heads_of(c):
             value = v_ref[:, columns(h)]
-            split = jnp.concatenate(halves(a_s[h]), axis=1)
-            later = dot(fk[h], split, (1, 0))
-            vg_ref[:, columns(h)] = vg_ref[:, columns(h)] + beyond * (later[:, :DH] + later[:, DH:])
-            from_later = dot(jnp.concatenate([value, value], axis=1), split, (1, 1))
+            adj = a_s[h].astype(BF)
+            later = dot(fk[h], adj, (1, 0))
+            vg_ref[:, columns(h)] = vg_ref[:, columns(h)] + beyond * later
+            from_later = dot(value, adj, (1, 1))
             hn_s[h] = hn_s[h] + beyond_f * from_later
 
     def key_side(c, total):
         for h in heads_of(c):
             key = k_ref[:, columns(h)]
             grad_fk = hn_s[h] + beyond_f * drift_s[h : h + 1, :F]
-            grad_pk = (grad_fk * (1.0 + dot(key, weight, (1, 1)))).astype(BF)
+            grad_pk = (grad_fk * slope_k[h]).astype(BF)
             kg_ref[:, columns(h)] = dot(grad_pk, weight, (1, 0))
             total = total + dot(grad_pk, key, (0, 0))
         return total
@@ -408,7 +405,10 @@
         scratch_shapes=[
             pltpu.VMEM((H, tokens, F), BF),
             pltpu.VMEM((H, tokens, F), BF),
+            pltpu.VMEM((H, tokens, F), F32),
+            pltpu.VMEM((H, tokens, F), F32),
             pltpu.VMEM((H, tokens, tokens), BF),
+            pltpu.VMEM((H, tokens, DH), BF),
             pltpu.VMEM((tokens, wide), F32),
             pltpu.VMEM((H, F, DH), F32),
             pltpu.VMEM((H, F, DH), F32),
@@ -437,10 +437,10 @@
         compiler_params=pltpu.CompilerParams(
             collective_id=0, has_side_effects=True, vmem_limit_bytes=LIMIT),
     )(doc_ids, q, k, v, g, feat_weight.T)
-    cols = pl.BlockSpec((tokens, wide // 4), lambda i: (0, i))
+    cols = pl.BlockSpec((tokens, wide // 8), lambda i: (0, i))
     placed = pl.pallas_call(
         hand_on,
-        grid=(4,),
+        grid=(8,),
         in_specs=[cols] * 4,
         out_specs=[cols] * 4,
         out_shape=[shape((tokens, wide), F32)] * 4,

time: 102 us -> 104 us (1.020)
  Pallas kernels: 99.3 us -> 101 us
    pallas_call x1, Pallas kernels: 4.7 us -> 6.63 us  [shards(): pl.pallas_call(hand_on, grid=(8,), in_specs=[cols] * 4, out_specs=[cols]...]
where the time goes in v4:
time: 104 us; the launch traced here: 102 us
  Pallas kernels  101 us (97%)
    pallas_call x1, Pallas kernels, shards(): pl.pallas_call(functools.partial(kernel, n, dp, group), in_specs=[pl.Bloc...  94.3 us
    pallas_call x1, Pallas kernels, shards(): pl.pallas_call(hand_on, grid=(8,), in_specs=[cols] * 4, out_specs=[cols]...  6.63 us

profile of v4, /device:TPU:0, one launch (start us, length us, event | category | flops | bytes accessed | tf_op | source)
XLA Modules:
  0.0 102.2 jit_solution(6019291361150192336)
XLA Ops:
  0.6 94.3 %shard_map.101 = (f32[128,2048]{1,0:T(8,128)}, f32[128,2048]{1,0:T(8,128)}, f32[128,2048]{1,0:T(8,128)}, f32[128,2048]{1,0:T(8,128)}, f32[160,128]{1,0:T(8,128)}) custom-call(s32[1,2]{1,0:T(1,128)} %doc_ref.1, bf16[128,2048]{1,0:T(8,128)(2,1)} %bitcast.10, bf16[128,2048]{1,0:T(8,128)(2,1)} %bitcast.11, bf16[128,2048]{1,0:T(8,128)(2,1)} %bitcast.12, ...), custom_call_target="tpu_custom_call" | custom-call | tf_op jit(solution)/shard_map/pallas_call | solution.py:400
  95.0 0.0 copy-start
  95.0 6.6 %shard_map.102 = (f32[128,2048]{1,0:T(8,128)}, f32[128,2048]{1,0:T(8,128)}, f32[128,2048]{1,0:T(8,128)}, f32[128,2048]{1,0:T(8,128)}) custom-call(f32[128,2048]{1,0:T(8,128)} %get-tuple-element.14.refs_0_, f32[128,2048]{1,0:T(8,128)} %get-tuple-element.15.refs_1_, f32[128,2048]{1,0:T(8,128)} %get-tuple-element.16.refs_2_, f32[128,2048]{1,0:T(8,128)} %get-tuple-element.17.refs_3_), custom_call_target="tpu_custom_call" | custom-call | tf_op jit(solution)/shard_map/pallas_call | solution.py:441
  101.6 0.0 copy-done
  101.6 0.6 copy.12
Async XLA Ops:
  95.0 6.6 %copy-start = (f32[160,128]{1,0:T(8,128)S(1)}, f32[160,128]{1,0:T(8,128)}, u32[]{:S(2)}) copy-start(f32[160,128]{1,0:T(8,128)} %get-tuple-element.22) | copy-start | bytes 245764
